TPU v7x, 256 devices: a whole 4x4x8 slice. The times are simulated.
256 devices in a mesh: grp: 16 (over y_hi, x, core), tok: 16 (over y_lo, z).
Axes of the slice: x: 4, y: 4 (y_hi: 2, y_lo: 2; y = y_hi * 2 + y_lo), z: 8, core: 2. Of those that a mesh axis runs over, the one named last changes fastest.
Arguments:
- tokens: bfloat16 [16, 2048, 4096], P('grp', 'tok'), may hold values from -6 to 6
- modulation: float32 [2, 4096], replicated, may hold values from -3 to 3
- triple_weight: bfloat16 [4096, 3, 2048], P(None, None, 'tok'), may hold values from -2.25 to 2.25
- out_weight: bfloat16 [2048, 4096], P(None, 'tok'), may hold values from -0.125 to 0.125
- gate: float32 [4096], P('tok'), may hold values from -8 to 8
- latent_weight: bfloat16 [4096, 128], replicated, may hold values from -0.09375 to 0.09375
- conv_weight: bfloat16 [3, 3, 3, 128, 256], replicated, may hold values from -0.109375 to 0.109375
- conv_bias: float32 [256], replicated, may hold values from -3 to 3
- res_weight: bfloat16 [3, 3, 3, 256, 256], replicated, may hold values from -0.078125 to 0.078125
- res_bias: float32 [256], replicated, may hold values from -3 to 3
Outputs:
- upsampled: bfloat16 [16, 128, 64, 256], P(None, 'grp', 'tok')
All inputs are finite; a program needn't handle non-finite values.
Results may differ from a plain program's by a relative error of at most 0.018.
Values may be sent and summed in bfloat16 or wider, within the bound.
A program may use at most 128 MiB of HBM per device.

v0:
```python
import jax
import jax.numpy as jnp
from jax import lax
from jax.sharding import PartitionSpec as P

HEAD_DIM = 128
HB = 4
WC = 2


def extended_2(block, sides, width):
    for axis, dim in sides:
        count = lax.axis_size(axis)
        forward = [(i, i + 1) for i in range(count - 1)]
        backward = [(target, source) for source, target in forward]
        low = lax.ppermute(
            lax.slice_in_dim(block, block.shape[dim] - width, None, axis=dim), axis, forward
        )
        high = lax.ppermute(lax.slice_in_dim(block, 0, width, axis=dim), axis, backward)
        block = jnp.concatenate([low, block, high], axis=dim)
    return block


def stencil(extended, weight):
    frames = extended.shape[0]
    rows = extended.shape[1] - 2
    cols = extended.shape[2] - 2
    padded = jnp.pad(extended, ((1, 1), (0, 0), (0, 0), (0, 0)))
    shifted = [
        padded[depth : depth + frames, across : across + rows, along : along + cols]
        for depth in range(3)
        for across in range(3)
        for along in range(3)
    ]
    stacked = jnp.concatenate(shifted, axis=-1).reshape(frames * rows * cols, -1)
    result = jnp.dot(
        stacked, weight.reshape(-1, weight.shape[-1]), preferred_element_type=jnp.float32
    )
    return result.reshape(frames, rows, cols, weight.shape[-1])


def rimmed(field):
    return extended_2(field, (("grp", 1), ("tok", 2)), 1)


def shards(
    tokens,
    modulation,
    triple_weight,
    out_weight,
    gate,
    latent_weight,
    conv_weight,
    conv_bias,
    res_weight,
    res_bias,
):
    n_tok = lax.axis_size("tok")
    own_rows = tokens[0]
    floats = own_rows.astype(jnp.float32)
    normed = floats * lax.rsqrt(jnp.mean(floats * floats, axis=-1, keepdims=True) + 1e-06)
    modulated = (normed * (1.0 + modulation[1]) + modulation[0]).astype(jnp.bfloat16)
    local_weight = triple_weight.reshape(triple_weight.shape[0], -1)
    triples = jnp.dot(
        lax.all_gather(modulated, "tok", axis=0, tiled=True),
        local_weight,
        preferred_element_type=jnp.float32,
    ).astype(jnp.bfloat16)
    length = triples.shape[0]
    width = triple_weight.shape[2]
    local_heads = width // HEAD_DIM
    triples = triples.reshape(length, 3, local_heads, HEAD_DIM)
    scores = jnp.einsum(
        "qhd,khd->hqk", triples[:, 0], triples[:, 1], preferred_element_type=jnp.float32
    ) * HEAD_DIM ** (-0.5)
    row_max = jnp.max(scores, axis=-1, keepdims=True)
    weights = jnp.exp(scores - row_max)
    probs = (weights / jnp.sum(weights, axis=-1, keepdims=True)).astype(jnp.bfloat16)
    attended = jnp.einsum("hqk,khd->qhd", probs, triples[:, 2], preferred_element_type=jnp.float32)
    attended = attended.astype(jnp.bfloat16).reshape(length, width)
    projected = jnp.dot(
        lax.all_gather(attended, "tok", axis=1, tiled=True),
        out_weight,
        preferred_element_type=jnp.float32,
    )
    branch = (gate * projected).astype(jnp.bfloat16)
    full_cols = n_tok * WC
    returned = lax.all_to_all(branch, "tok", split_axis=0, concat_axis=1, tiled=True)
    latent = jnp.dot(own_rows, latent_weight, preferred_element_type=jnp.float32) + jnp.dot(
        returned, latent_weight, preferred_element_type=jnp.float32
    )
    latent = latent.astype(jnp.bfloat16).reshape(1, HB, full_cols, latent_weight.shape[1])
    tile = lax.all_to_all(latent, "tok", split_axis=2, concat_axis=0, tiled=True)
    coarse = jax.nn.silu(stencil(rimmed(tile), conv_weight) + conv_bias).astype(jnp.bfloat16)
    upscaled = jnp.repeat(jnp.repeat(coarse, 2, axis=1), 2, axis=2)
    border = rimmed(upscaled)
    result = jax.nn.silu(upscaled.astype(jnp.float32) + stencil(border, res_weight) + res_bias)
    return result.astype(jnp.bfloat16)


def solution(mesh):
    placed = (
        P("grp", "tok", None),
        P(),
        P(None, None, "tok"),
        P(None, "tok"),
        P("tok"),
        P(),
        P(),
        P(),
        P(),
        P(),
    )
    return jax.shard_map(
        shards, mesh=mesh, in_specs=placed, out_specs=P(None, "grp", "tok", None), check_vma=False
    )
```

profile of v0, /device:TPU:7, one launch (start us, length us, event | category | flops | bytes accessed | tf_op | source)
XLA Modules:
  0.0 451.3 jit_solution(12882700306745127066)
XLA Ops:
  9.2 2.6 fusion.15
  11.8 4.7 %copy.18 = bf16[4096,3,128]{0,2,1:T(8,128)(2,1)} copy(bf16[4096,3,128]{2,0,1:T(8,128)(2,1)} %param.12) | data formatting | bytes 6291456 | tf_op args[2]
  16.6 183.6 %all-gather.4.cloned.1.call-done = bf16[2048,4096]{1,0:T(8,128)(2,1)} async-done(((bf16[128,4096]{1,0:T(8,128)(2,1)}), bf16[2048,4096]{1,0:T(8,128)(2,1)}) %all-gather.4.cloned.1.call-update) | async-done | bytes 16777232 | tf_op jit(solution)/shard_map/all_gather | solution.py:65
  200.1 11.2 %convolution_convert_fusion = bf16[2048,384]{0,1:T(8,128)(2,1)S(1)} fusion(bf16[2048,4096]{1,0:T(8,128)(2,1)} %all-gather.4.cloned.1.call-done, bf16[4096,384]{0,1:T(8,128)(2,1)} %bitcast.78), kind=kOutput, calls=%fused_computation.7 | convolution fusion | flops 6443237376 | bytes 21495808 | tf_op jit(solution)/shard_map/dot_general | solution.py:64
  211.3 8.1 %multiply_reduce_fusion = (f32[2048]{0:T(1024)S(1)}, f32[2048,2048]{0,1:T(8,128)}) fusion(bf16[2048,3,1,128]{0,3,1,2:T(8,128)(2,1)S(1)} %bitcast.86), kind=kOutput, calls=%fused_computation.2 | convolution fusion | flops 1082128384 | bytes 17833984 | tf_op jit(solution)/shard_map/qhd,khd->hqk/dot_general | solution.py:73
  219.4 8.6 %fusion = f32[2048]{0:T(1024)S(1)} fusion(f32[2048,2048]{0,1:T(8,128)} %get-tuple-element.20, f32[2048]{0:T(1024)S(1)} %get-tuple-element.19), kind=kLoop, calls=%fused_computation.3 | loop fusion | flops 12580864 | bytes 16793600 | tf_op jit(solution)/shard_map/reduce_sum | solution.py:78
  228.0 8.6 %fusion.11 = bf16[2048,1,128]{0,2,1:T(8,128)(2,1)} fusion(f32[2048,2048]{0,1:T(8,128)} %get-tuple-element.20, f32[2048]{0:T(1024)S(1)} %fusion, f32[2048]{0:T(1024)S(1)} %get-tuple-element.19, bf16[2048,3,1,128]{0,3,1,2:T(8,128)(2,1)S(1)} %bitcast.87), kind=kOutput, calls=%fused_computation.15 | convolution fusion | flops 1090781184 | bytes 17842176 | tf_op jit(solution)/shard_map/hqk,khd->qhd/dot_general | solution.py:79
  236.6 98.8 %all-gather.6.cloned.1.call-done = bf16[2048,1,2048]{0,2,1:T(8,128)(2,1)} async-done(((bf16[2048,1,128]{0,2,1:T(8,128)(2,1)}), bf16[2048,1,2048]{0,2,1:T(8,128)(2,1)}) %all-gather.6.cloned.1.call-update) | async-done | bytes 8388624 | tf_op jit(solution)/shard_map/all_gather | solution.py:82
  335.4 7.2 %fusion.7 = bf16[2048,256]{1,0:T(8,128)(2,1)} fusion(bf16[2048,256]{1,0:T(8,128)(2,1)} %param.13, bf16[2048,1,2048]{0,2,1:T(8,128)(2,1)} %all-gather.6.cloned.1.call-done, f32[256]{0:T(256)S(1)} %copy-done.1), kind=kOutput, calls=%fused_computation.13 | convolution fusion | flops 2148532224 | bytes 10486784 | tf_op jit(solution)/shard_map/dot_general | solution.py:81
  342.6 2.3 copy.19
  344.9 4.3 all-to-all-start
  349.2 2.6 fusion.19
  351.8 23.0 %all-to-all-done = bf16[16,128,256]{1,2,0:T(8,128)(2,1)} async-done(((bf16[16,128,256]{1,2,0:T(8,128)(2,1)}), bf16[16,128,256]{1,2,0:T(8,128)(2,1)}, u32[]{:S(2)}, u32[]{:S(2)}) %all-to-all-start) | async-done | bytes 1048608 | tf_op jit(solution)/shard_map/all_to_all | solution.py:88
  374.8 2.0 fusion.18
  376.8 13.2 %all_to_all.37 = bf16[1,4,32,128]{3,1,0,2:T(4,128)(2,1)S(1)} all-to-all(bf16[1,4,32,128]{3,1,0,2:T(4,128)(2,1)S(1)} %copy.20), channel_id=1, replica_groups=mesh['grp'=16,'tok'=16] {'tok'}, dimensions={2} | all-to-all | bytes 65536 | tf_op jit(solution)/shard_map/all_to_all | solution.py:93
  390.1 6.2 %collective-permute-start = (bf16[16,1,2,128]{3,0,2,1:T(8,128)(2,1)S(1)}, bf16[16,1,2,128]{3,0,2,1:T(8,128)(2,1)S(1)}, u32[]{:S(2)}, u32[]{:S(2)}) collective-permute-start(bf16[16,1,2,128]{3,0,2,1:T(8,128)(2,1)S(1)} %get-tuple-element.15), channel_id=1, source_target_pairs={{0,16},{16,32},{32,48},{48,64},{64,80},{80,96},{96,112},{112,128},... | collective-permute-start | bytes 24584 | tf_op jit(solution)/shard_map/ppermute | solution.py:16
  398.2 6.6 %collective-permute-done.1 = bf16[16,1,2,128]{3,0,2,1:T(8,128)(2,1)S(1)} collective-permute-done((bf16[16,1,2,128]{3,0,2,1:T(8,128)(2,1)S(1)}, bf16[16,1,2,128]{3,0,2,1:T(8,128)(2,1)S(1)}, u32[]{:S(2)}, u32[]{:S(2)}) %collective-permute-start.1) | collective-permute-done | bytes 8224 | tf_op jit(solution)/shard_map/ppermute | solution.py:19
  404.9 2.4 collective-permute-start.2
  408.7 3.3 collective-permute-done.3
  417.9 3.4 collective-permute-start.4
  423.2 7.3 %collective-permute-done.5 = bf16[16,1,4,256]{3,1,2,0:T(2,128)(2,1)S(1)} collective-permute-done((bf16[16,1,4,256]{3,1,2,0:T(2,128)(2,1)S(1)}, bf16[16,1,4,256]{3,1,2,0:T(2,128)(2,1)S(1)}, u32[]{:S(2)}, u32[]{:S(2)}) %collective-permute-start.5) | collective-permute-done | bytes 32800 | tf_op jit(solution)/shard_map/ppermute | solution.py:19
  430.7 2.2 collective-permute-start.6
  434.7 3.8 collective-permute-done.7
  441.6 2.1 multiply_convert_fusion
  (94 shorter events, 19.4 us)
Async XLA Ops:
  6.5 435.0 %copy-start = (bf16[3,3,3,256,256]{4,3,2,1,0:T(8,128)(2,1)S(1)}, bf16[3,3,3,256,256]{4,3,2,1,0:T(8,128)(2,1)}, u32[]{:S(2)}) copy-start(bf16[3,3,3,256,256]{4,3,2,1,0:T(8,128)(2,1)} %param.18) | copy-start | bytes 10616836
  6.5 193.6 %all-gather.4.cloned.1.call-start = ((), (), s32[]{:S(2)}) async-start(), calls=%async_computation.2 | async-start | bytes 17825792 | tf_op jit(solution)/shard_map/all_gather | solution.py:65
  11.8 323.6 %all-gather.6.cloned.1.call-start = ((), (), s32[]{:S(2)}) async-start(), calls=%async_computation.3 | async-start | bytes 8912896 | tf_op jit(solution)/shard_map/all_gather | solution.py:82
  228.0 107.4 %copy-start.1 = (f32[256]{0:T(256)S(1)}, f32[256]{0:T(256)}, u32[]{:S(2)}) copy-start(f32[256]{0:T(256)} %param.14) | copy-start | bytes 3076
  342.6 70.0 %copy-start.2 = (f32[256]{0:T(256)S(1)}, f32[256]{0:T(256)}, u32[]{:S(2)}) copy-start(f32[256]{0:T(256)} %param.17) | copy-start | bytes 3076
  344.9 29.9 %all-to-all-start = ((bf16[16,128,256]{1,2,0:T(8,128)(2,1)}), bf16[16,128,256]{1,2,0:T(8,128)(2,1)}, u32[]{:S(2)}, u32[]{:S(2)}) async-start(bf16[16,128,256]{1,2,0:T(8,128)(2,1)} %copy.19), calls=%async_computation | async-start | bytes 2097152 | tf_op jit(solution)/shard_map/all_to_all | solution.py:88
  390.1 8.1 %collective-permute-start = (bf16[16,1,2,128]{3,0,2,1:T(8,128)(2,1)S(1)}, bf16[16,1,2,128]{3,0,2,1:T(8,128)(2,1)S(1)}, u32[]{:S(2)}, u32[]{:S(2)}) collective-permute-start(bf16[16,1,2,128]{3,0,2,1:T(8,128)(2,1)S(1)} %get-tuple-element.15), channel_id=1, source_target_pairs={{0,16},{16,32},{32,48},{48,64},{64,80},{80,96},{96,112},{112,128},... | collective-permute-start | bytes 24584 | tf_op jit(solution)/shard_map/ppermute | solution.py:16
  396.3 8.6 %collective-permute-start.1 = (bf16[16,1,2,128]{3,0,2,1:T(8,128)(2,1)S(1)}, bf16[16,1,2,128]{3,0,2,1:T(8,128)(2,1)S(1)}, u32[]{:S(2)}, u32[]{:S(2)}) collective-permute-start(bf16[16,1,2,128]{3,0,2,1:T(8,128)(2,1)S(1)} %get-tuple-element.16), channel_id=1, source_target_pairs={{16,0},{32,16},{48,32},{64,48},{80,64},{96,80},{112,96},{128,112},... | collective-permute-start | bytes 24584 | tf_op jit(solution)/shard_map/ppermute | solution.py:19
  404.9 3.7 collective-permute-start.2
  407.3 4.6 %collective-permute-start.3 = (bf16[16,6,1,128]{3,0,2,1:T(8,128)(2,1)S(1)}, bf16[16,6,1,128]{3,0,2,1:T(8,128)(2,1)S(1)}, u32[]{:S(2)}, u32[]{:S(2)}) collective-permute-start(bf16[16,6,1,128]{3,0,2,1:T(8,128)(2,1)S(1)} %get-tuple-element.14), channel_id=1, source_target_pairs={{1,0},{2,1},{3,2},{4,3},{5,4},{6,5},{7,6},{8,7},{9,8},{10,9},{11,1... | collective-permute-start | bytes 73736 | tf_op jit(solution)/shard_map/ppermute | solution.py:19
  417.9 5.3 %collective-permute-start.4 = (bf16[16,1,4,256]{3,1,2,0:T(2,128)(2,1)S(1)}, bf16[16,1,4,256]{3,1,2,0:T(2,128)(2,1)S(1)}, u32[]{:S(2)}, u32[]{:S(2)}) collective-permute-start(bf16[16,1,4,256]{3,1,2,0:T(2,128)(2,1)S(1)} %get-tuple-element.9), channel_id=1, source_target_pairs={{0,16},{16,32},{32,48},{48,64},{64,80},{80,96},{96,112},{112,128},... | collective-permute-start | bytes 98312 | tf_op jit(solution)/shard_map/ppermute | solution.py:16
  421.3 9.2 %collective-permute-start.5 = (bf16[16,1,4,256]{3,1,2,0:T(2,128)(2,1)S(1)}, bf16[16,1,4,256]{3,1,2,0:T(2,128)(2,1)S(1)}, u32[]{:S(2)}, u32[]{:S(2)}) collective-permute-start(bf16[16,1,4,256]{3,1,2,0:T(2,128)(2,1)S(1)} %get-tuple-element.10), channel_id=1, source_target_pairs={{16,0},{32,16},{48,32},{64,48},{80,64},{96,80},{112,96},{128,112},... | collective-permute-start | bytes 98312 | tf_op jit(solution)/shard_map/ppermute | solution.py:19
  430.7 4.1 collective-permute-start.6
  432.8 5.7 %collective-permute-start.7 = (bf16[16,10,1,256]{3,1,2,0:T(8,128)(2,1)S(1)}, bf16[16,10,1,256]{3,1,2,0:T(8,128)(2,1)S(1)}, u32[]{:S(2)}, u32[]{:S(2)}) collective-permute-start(bf16[16,10,1,256]{3,1,2,0:T(8,128)(2,1)S(1)} %get-tuple-element.8), channel_id=1, source_target_pairs={{1,0},{2,1},{3,2},{4,3},{5,4},{6,5},{7,6},{8,7},{9,8},{10,9},{11,1... | collective-permute-start | bytes 245768 | tf_op jit(solution)/shard_map/ppermute | solution.py:19
  439.1 2.5 copy-start.3
Sparse Core Ops, SparseCore 0:
  11.9 188.1 all-gather.3
  236.7 98.6 all-gather.5
where the time goes:
time: 454 us; the launch traced here: 451 us
  waiting for transfers between devices  327 us (72%)
  matrix products  43.6 us (10%)
  starting transfers between devices  25 us (6%)
  other arithmetic  15.4 us (3%)
  between operations  14 us (3%)
  local copies, waits for them, and re-layouts  13.2 us (3%)
  blocking collectives  13.2 us (3%)
    all_gather x1, waiting for transfers between devices, shards(): lax.all_gather(modulated, 'tok', axis=0, tiled=True)  184 us
    all_gather x1, waiting for transfers between devices, shards(): lax.all_gather(attended, 'tok', axis=1, tiled=True)  98.8 us
    all_to_all x1, waiting for transfers between devices, shards(): lax.all_to_all(branch, 'tok', split_axis=0, concat_axis=1, tiled=True)  23 us
    ppermute x4, waiting for transfers between devices, extended_2(): lax.ppermute(lax.slice_in_dim(block, 0, width, axis=dim), axis, backward)  21 us
    ppermute x4, starting transfers between devices, extended_2(): lax.ppermute(lax.slice_in_dim(block, block.shape[dim] - width, None, axis...  14.2 us
    all_to_all x1, blocking collectives, shards(): lax.all_to_all(latent, 'tok', split_axis=2, concat_axis=0, tiled=True)  13.2 us
    dot_general x1, matrix products, shards(): jnp.dot(lax.all_gather(modulated, 'tok', axis=0, tiled=True), local_weigh...  11.2 us
  transfers between devices with their start and end apart: 11, of which 8 were waited for; matrix products, arithmetic and copies ran while one was open for 2% of the time, Pallas kernels for 0%

commit v1 on v0

v1 whole, which is shorter than its diff:
```python
import math

import jax
import jax.numpy as jnp
from jax import lax
from jax.experimental import pallas as pl
from jax.experimental.pallas import tpu as pltpu
from jax.sharding import PartitionSpec as P

MESH = pl.DeviceIdType.MESH
F32 = jnp.float32
BF16 = jnp.bfloat16

D = 4096
HD = 128
FR = 16
BLK = 128
SUBS = 2
SUB = BLK // SUBS
LAT = 128
CH = 256
NZ = 8
W_CUT = 1408
EXP_SCALE = HD ** (-0.5) * math.log2(math.e)


def kernel(
    tok_ref, mod_ref, w_hbm, ow_hbm, gate_ref, lw_hbm, cw_hbm, cb_ref, rw_hbm, rb_ref,
    out_ref,
    xall, xown, wv, lw, ow, cw, rw, qs, kt, v2, radd, rmine, rbuf, mrecv, msend, mfull,
    lsend, lrecv, ext, coarse, cols2,
    local_sem, wloc_sem, swx_send, swx_recv, sww_send, sww_recv, swr_send, swr_recv,
    ring_send, ring_recv, sib_send, sib_recv, m_send, m_recv, mx_send, mx_recv,
    l_send, l_recv, h_send, h_recv,
):
    g = lax.axis_index("grp")
    t = lax.axis_index("tok")
    n_x = lax.axis_size("grp") // 4
    n_g = lax.axis_size("grp")
    core = lax.rem(g, 2)
    pair = g - core
    x = lax.rem(g // 2, n_x)
    y_hi = g // (2 * n_x)
    y_lo = t // NZ
    z = lax.rem(t, NZ)
    swapped = core != y_lo
    head = core * NZ + z
    mate_grp = pair + y_lo
    far_grp = (1 - y_hi) * (2 * n_x) + x * 2 + y_lo
    mate_tok = head
    sib_grp = pair + 1 - core
    up_tok = y_lo * NZ + lax.rem(z + 1, NZ)
    down_tok = y_lo * NZ + lax.rem(z + NZ - 1, NZ)
    outer = g + 2 * core - 1
    has_outer = jnp.logical_and(outer >= 0, outer < n_g)

    ext[...] = jnp.zeros_like(ext)

    barrier = pltpu.get_barrier_semaphore()

    def greet(grp, tok):
        pl.semaphore_signal(barrier, inc=1, device_id=(grp, tok), device_id_type=MESH)

    def greet_row(step, carry):
        other = lax.rem(t + step, FR)

        @pl.when(step > 0)
        def _():
            greet(g, other)

        greet(sib_grp, other)
        return carry

    lax.fori_loop(0, FR, greet_row, 0)
    for step in range(1, 4):
        greet(y_hi * (2 * n_x) + lax.rem(x + step, n_x) * 2 + core, t)

    @pl.when(swapped)
    def _():
        greet(far_grp, mate_tok)

    @pl.when(has_outer)
    def _():
        greet(outer, t)

        @pl.when(t > 0)
        def _():
            greet(outer, t - 1)

        @pl.when(t < FR - 1)
        def _():
            greet(outer, t + 1)

    guests = 2 * FR - 1 + 3 + jnp.where(swapped, 1, 0) + jnp.where(
        has_outer, 1 + jnp.where(t > 0, 1, 0) + jnp.where(t < FR - 1, 1, 0), 0
    )

    load_lw = pltpu.make_async_copy(lw_hbm, lw, local_sem.at[0])
    load_ow = pltpu.make_async_copy(ow_hbm.at[core, :, x], ow, local_sem.at[1])
    load_cw = pltpu.make_async_copy(cw_hbm, cw, local_sem.at[2])
    load_rw = pltpu.make_async_copy(rw_hbm, rw, local_sem.at[3])
    load_lw.start()
    load_ow.start()
    load_w = pltpu.make_async_copy(w_hbm, wv, wloc_sem.at[0])

    @pl.when(jnp.logical_not(swapped))
    def _():
        load_w.start()

    load_cw.start()
    load_rw.start()

    v2[:, HD:] = jnp.ones((v2.shape[0], HD), BF16)
    radd[...] = jnp.zeros_like(radd)

    def rows_of(sub):
        return pl.ds(sub * SUB, SUB)

    def swap_x(sub):
        return pltpu.make_async_remote_copy(
            src_ref=xown.at[rows_of(sub)],
            dst_ref=xall.at[t, rows_of(sub)],
            send_sem=swx_send.at[sub],
            recv_sem=swx_recv.at[sub],
            device_id=(mate_grp, mate_tok),
            device_id_type=MESH,
        )

    def wait_swap_x(sub):
        pltpu.make_async_copy(
            xall.at[head, rows_of(sub)], xall.at[head, rows_of(sub)], swx_recv.at[sub]
        ).wait()

    def swap_w(part):
        rows = pl.ds(0, W_CUT) if part == 0 else pl.ds(W_CUT, D - W_CUT)
        return pltpu.make_async_remote_copy(
            src_ref=w_hbm.at[rows],
            dst_ref=wv.at[rows],
            send_sem=sww_send.at[part],
            recv_sem=sww_recv.at[part],
            device_id=(mate_grp if part == 0 else far_grp, mate_tok),
            device_id_type=MESH,
        )

    def swap_r():
        return pltpu.make_async_remote_copy(
            src_ref=rmine,
            dst_ref=rbuf,
            send_sem=swr_send.at[0],
            recv_sem=swr_recv.at[0],
            device_id=(mate_grp, mate_tok),
            device_id_type=MESH,
        )

    def ring(way, step, sub):
        origin = lax.rem(z + (NZ - step if way == 0 else step), NZ)
        block = xall.at[core * NZ + origin, rows_of(sub)]
        return pltpu.make_async_remote_copy(
            src_ref=block,
            dst_ref=block,
            send_sem=ring_send.at[way, step, sub],
            recv_sem=ring_recv.at[way, step, sub],
            device_id=(g, up_tok if way == 0 else down_tok),
            device_id_type=MESH,
        )

    def wait_ring(way, step, sub):
        origin = lax.rem(z + (NZ - step if way == 0 else step), NZ)
        block = xall.at[core * NZ + origin, rows_of(sub)]
        pltpu.make_async_copy(block, block, ring_recv.at[way, step - 1, sub]).wait()

    def share(origin, sub):
        block = xall.at[core * NZ + origin, rows_of(sub)]
        return pltpu.make_async_remote_copy(
            src_ref=block,
            dst_ref=block,
            send_sem=sib_send.at[origin, sub],
            recv_sem=sib_recv.at[origin, sub],
            device_id=(sib_grp, t),
            device_id_type=MESH,
        )

    def origin_of(way, step):
        return lax.rem(z + (NZ - step if way == 0 else step), NZ)

    reach = (4 - core, 3 + core)

    load_lw.wait()

    new = lax.broadcasted_iota(jnp.int32, (BLK, BLK), 0)
    old = lax.broadcasted_iota(jnp.int32, (BLK, BLK), 1)
    source = (lax.rem(new // 2, 4)) * 32 + (new // 8) * 2 + lax.rem(new, 2)
    pick = jnp.where(old == source, 1.0, 0.0).astype(BF16)

    def prepare(sub):
        own = jnp.dot(
            pick[sub * SUB : (sub + 1) * SUB], tok_ref[...], preferred_element_type=F32
        )
        rmine[rows_of(sub), :] = jnp.dot(own.astype(BF16), lw[...], preferred_element_type=F32)
        scale = lax.rsqrt(jnp.mean(own * own, axis=-1, keepdims=True) + 1e-06)
        made = (own * scale * (1.0 + mod_ref[1:2, :]) + mod_ref[0:1, :]).astype(BF16)

        @pl.when(swapped)
        def _():
            xown[rows_of(sub), :] = made

        @pl.when(jnp.logical_not(swapped))
        def _():
            xall[head, rows_of(sub), :] = made

    prepare(0)
    pl.semaphore_wait(barrier, guests)

    @pl.when(swapped)
    def _():
        swap_x(0).start()
        swap_w(1).start()

    @pl.when(jnp.logical_not(swapped))
    def _():
        ring(0, 0, 0).start()
        ring(1, 0, 0).start()
        share(z, 0).start()

    prepare(1)

    @pl.when(swapped)
    def _():
        swap_x(1).start()
        swap_w(0).start()
        swap_r().start()
        wait_swap_x(0)
        ring(0, 0, 0).start()
        ring(1, 0, 0).start()
        share(z, 0).start()
        wait_swap_x(1)

    ring(0, 0, 1).start()
    ring(1, 0, 1).start()
    share(z, 1).start()

    load_ow.wait()
    scaled = (ow[...].astype(F32) * gate_ref[...]).astype(BF16).reshape(NZ * 32, 256)
    cols = pl.ds(pl.multiple_of(t * 256, 256), 256)
    part = jnp.dot(scaled, lw[cols, :], preferred_element_type=F32)
    msend[...] = part.astype(BF16).reshape(NZ, 32, LAT)

    def fold_copy(other):
        return pltpu.make_async_remote_copy(
            src_ref=msend.at[lax.rem(other, NZ)],
            dst_ref=mrecv.at[t],
            send_sem=m_send.at[other],
            recv_sem=m_recv.at[t],
            device_id=(g, other),
            device_id_type=MESH,
        )

    mrecv[t] = msend[z]

    def fold_send(step, carry):
        fold_copy(lax.rem(t + step, FR)).start()
        return carry

    lax.fori_loop(1, FR, fold_send, 0)

    def fold_wait(step, carry):
        other = lax.rem(t + step, FR)
        pltpu.make_async_copy(mrecv.at[other], mrecv.at[other], m_recv.at[other]).wait()
        return carry

    def fold_sent(step, carry):
        fold_copy(lax.rem(t + step, FR)).wait_send()
        return carry

    def fold_rows(which):
        return mfull.at[pl.ds(pl.multiple_of(which * 32, 32), 32)]

    def spread(step):
        return pltpu.make_async_remote_copy(
            src_ref=fold_rows(x),
            dst_ref=fold_rows(x),
            send_sem=mx_send.at[step],
            recv_sem=mx_recv.at[x],
            device_id=(y_hi * (2 * n_x) + lax.rem(x + step, n_x) * 2 + core, t),
            device_id_type=MESH,
        )

    def project(kind, origin):
        slot = kind * NZ + origin
        triple = jnp.dot(xall[slot], wv[...], preferred_element_type=F32)
        qs[pl.ds(slot, BLK, stride=FR), :] = triple[:, :HD]
        at = pl.ds(pl.multiple_of(slot * BLK, BLK), BLK)
        kt[:, at] = triple[:, HD : 2 * HD].T.astype(BF16)
        v2[at, :HD] = triple[:, 2 * HD :].astype(BF16)

    def project_sib(origin):
        for sub in range(SUBS):
            block = xall.at[(1 - core) * NZ + origin, rows_of(sub)]
            pltpu.make_async_copy(block, block, sib_recv.at[origin, sub]).wait()
        project(1 - core, origin)

    def forward(step):
        for sub in range(SUBS):
            for way in range(2):

                @pl.when(step <= reach[way])
                def _():
                    wait_ring(way, step, sub)

                    @pl.when(step < reach[way])
                    def _():
                        ring(way, step, sub).start()

                    share(origin_of(way, step), sub).start()

    def both(step, work):
        def go(way, carry):
            work(lax.rem(z + NZ + (2 * way - 1) * step, NZ))
            return carry

        lax.fori_loop(0, 2, go, 0)

    forward(1)

    @pl.when(jnp.logical_not(swapped))
    def _():
        load_w.wait()
        rbuf[...] = rmine[...]

    @pl.when(swapped)
    def _():
        pltpu.make_async_copy(wv.at[pl.ds(W_CUT, D - W_CUT)], wv.at[pl.ds(W_CUT, D - W_CUT)], sww_recv.at[1]).wait()
        pltpu.make_async_copy(wv.at[pl.ds(0, W_CUT)], wv.at[pl.ds(0, W_CUT)], sww_recv.at[0]).wait()
        pltpu.make_async_copy(rbuf, rbuf, swr_recv.at[0]).wait()

    def first(n, carry):
        project(core, lax.rem(z + NZ + lax.rem(n + 1, 3) - 1, NZ))
        return carry

    lax.fori_loop(0, 3, first, 0)
    project_sib(z)
    radd[pl.ds(head, BLK, stride=FR), :] = rbuf[...]
    lax.fori_loop(1, FR, fold_wait, 0)
    total = mrecv[0].astype(F32)
    for other in range(1, FR):
        total = total + mrecv[other].astype(F32)
    mfull[pl.ds(pl.multiple_of(x * 32, 32), 32), :] = total.astype(BF16)
    for step in range(1, 4):
        spread(step).start()

    forward(2)
    both(2, lambda origin: project(core, origin))
    both(1, project_sib)
    forward(3)
    both(3, lambda origin: project(core, origin))
    both(2, project_sib)
    both(3, project_sib)
    for step in range(1, 4):
        there = lax.rem(x + step, n_x)
        pltpu.make_async_copy(fold_rows(there), fold_rows(there), mx_recv.at[there]).wait()
    forward(4)
    last = lax.rem(z + 4, NZ)
    project(core, last)
    project_sib(last)

    home = pair + y_lo

    def latent_copy(target):
        return pltpu.make_async_remote_copy(
            src_ref=lsend.at[target],
            dst_ref=lrecv.at[head],
            send_sem=l_send.at[target],
            recv_sem=l_recv.at[head],
            device_id=(home, target),
            device_id_type=MESH,
        )

    def is_self(target):
        return jnp.logical_and(home == g, target == t)

    def attend(n, carry):
        two = lax.rem(n + t // 2 + 1, FR // 2)
        at = pl.ds(pl.multiple_of(two * 256, 256), 256)
        scores = jnp.dot(qs[at, :].astype(BF16), kt[...], preferred_element_type=F32)
        top = jnp.max(scores, axis=-1, keepdims=True)
        probs = jnp.exp2((scores - top) * EXP_SCALE).astype(BF16)
        summed = jnp.dot(probs, v2[...], preferred_element_type=F32)
        attended = (summed[:, :HD] / summed[:, HD:]).astype(BF16)
        latent = jnp.dot(attended, mfull[...], preferred_element_type=F32) + radd[at, :]
        pieces = latent.astype(BF16).reshape(2, BLK, LAT)
        lsend[pl.ds(pl.multiple_of(two * 2, 2), 2)] = pieces
        for half in range(2):
            target = two * 2 + half

            @pl.when(jnp.logical_not(is_self(target)))
            def _():
                latent_copy(target).start()

            @pl.when(is_self(target))
            def _():
                lrecv[head] = pieces[half]

        return carry

    lax.fori_loop(0, FR // 2, attend, 0)

    def latent_wait(n, carry):
        @pl.when(jnp.logical_not(jnp.logical_and(core == y_lo, n == head)))
        def _():
            pltpu.make_async_copy(lrecv.at[n], lrecv.at[n], l_recv.at[n]).wait()

        return carry

    lax.fori_loop(0, FR, latent_wait, 0)
    tile = lrecv[0].astype(F32)
    for n in range(1, FR):
        tile = tile + lrecv[n].astype(F32)
    ext[2:6, 2:4] = tile.astype(BF16).reshape(4, 2, FR, LAT)

    def halo(dg, dt):
        rows_src, rows_dst = {0: ((2, 4), (2, 4)), 1: ((4, 2), (0, 2)), -1: ((2, 2), (6, 2))}[dg]
        cols_dst = {0: 2, 1: 0, -1: 4}[dt]
        at = (dg + 1) * 3 + dt + 1
        return pltpu.make_async_remote_copy(
            src_ref=ext.at[pl.ds(*rows_src), pl.ds(2, 2)],
            dst_ref=ext.at[pl.ds(*rows_dst), pl.ds(cols_dst, 2)],
            send_sem=h_send.at[at],
            recv_sem=h_recv.at[at],
            device_id=(g + dg, t + dt),
            device_id_type=MESH,
        )

    def inside(dg, dt):
        ok = jnp.logical_and(g + dg >= 0, g + dg < n_g)
        return jnp.logical_and(ok, jnp.logical_and(t + dt >= 0, t + dt < FR))

    ways = [(dg, dt) for dg in (-1, 0, 1) for dt in (-1, 0, 1) if (dg, dt) != (0, 0)]
    for dg, dt in ways:

        @pl.when(inside(dg, dt))
        def _():
            halo(dg, dt).start()

    load_cw.wait()
    load_rw.wait()
    for dg, dt in ways:

        @pl.when(inside(-dg, -dt))
        def _():
            halo(dg, dt).wait_recv()

    def over_frames(three, rows):
        frame = lax.rem(lax.broadcasted_iota(jnp.int32, (rows, CH), 0), FR)
        before = pltpu.roll(three[0], 1, 0)
        after = pltpu.roll(three[2], rows - 1, 0)
        return (
            three[1]
            + jnp.where(frame > 0, before, 0.0)
            + jnp.where(frame < FR - 1, after, 0.0)
        )

    def silu(v):
        return v / (1.0 + jnp.exp(-v))

    views = [
        ext[b : b + 6, c : c + 4].reshape(24 * FR, LAT) for b in range(3) for c in range(3)
    ]
    cells = jnp.concatenate(views, axis=1)
    three = [jnp.dot(cells, cw[a], preferred_element_type=F32) for a in range(3)]
    made = silu(over_frames(three, 24 * FR) + cb_ref[...]).astype(BF16)
    coarse[...] = made.reshape(6, 4, FR, CH)

    @pl.when(g == 0)
    def _():
        coarse[0:1] = jnp.zeros((1, 4, FR, CH), BF16)

    @pl.when(g == n_g - 1)
    def _():
        coarse[5:6] = jnp.zeros((1, 4, FR, CH), BF16)

    @pl.when(t == 0)
    def _():
        coarse[:, 0:1] = jnp.zeros((6, 1, FR, CH), BF16)

    @pl.when(t == FR - 1)
    def _():
        coarse[:, 3:4] = jnp.zeros((6, 1, FR, CH), BF16)

    rows = 8 * FR
    for p in range(2):
        for q in range(2):
            for b in range(3):
                for c in range(3):
                    r0 = 1 + (p + b - 1) // 2
                    c0 = 1 + (q + c - 1) // 2
                    at = (p * 2 + q) * rows
                    k = (b * 3 + c) * CH
                    cols2[at : at + rows, k : k + CH] = coarse[
                        r0 : r0 + 4, c0 : c0 + 2
                    ].reshape(rows, CH)
    three = [jnp.dot(cols2[...], rw[a], preferred_element_type=F32) for a in range(3)]
    mixed = over_frames(three, 4 * rows)
    center = coarse[1:5, 1:3].reshape(rows, CH).astype(F32)
    for n in range(4):
        result = silu(center + mixed[n * rows : (n + 1) * rows] + rb_ref[...])
        out_ref[n] = result.astype(BF16).reshape(4, 2, FR, CH)

    for sub in range(SUBS):

        @pl.when(swapped)
        def _():
            swap_x(sub).wait_send()

        for way in range(2):
            for step in range(4):

                @pl.when(step < reach[way])
                def _():
                    ring(way, step, sub).wait_send()

        for origin in range(NZ):
            share(origin, sub).wait_send()

    @pl.when(swapped)
    def _():
        swap_w(0).wait_send()
        swap_w(1).wait_send()
        swap_r().wait_send()

    lax.fori_loop(1, FR, fold_sent, 0)
    for step in range(1, 4):
        spread(step).wait_send()

    def latent_sent(target, carry):
        @pl.when(jnp.logical_not(is_self(target)))
        def _():
            latent_copy(target).wait_send()

        return carry

    lax.fori_loop(0, FR, latent_sent, 0)
    for dg, dt in ways:

        @pl.when(inside(dg, dt))
        def _():
            halo(dg, dt).wait_send()


def shards(
    tokens,
    modulation,
    triple_weight,
    out_weight,
    gate,
    latent_weight,
    conv_weight,
    conv_bias,
    res_weight,
    res_bias,
):
    vmem = pl.BlockSpec(memory_space=pltpu.VMEM)
    hbm = pl.BlockSpec(memory_space=pl.ANY)
    dma = pltpu.SemaphoreType.DMA
    out = pl.pallas_call(
        kernel,
        out_shape=jax.ShapeDtypeStruct((4, 4, 2, FR, CH), BF16),
        in_specs=[vmem, vmem, hbm, hbm, vmem, hbm, hbm, vmem, hbm, vmem],
        out_specs=vmem,
        scratch_shapes=[
            pltpu.VMEM((FR, BLK, D), BF16),
            pltpu.VMEM((BLK, D), BF16),
            pltpu.VMEM((D, 3 * HD), BF16),
            pltpu.VMEM((D, LAT), BF16),
            pltpu.VMEM((NZ, 32, 256), BF16),
            pltpu.VMEM((3, 9 * LAT, CH), BF16),
            pltpu.VMEM((3, 9 * CH, CH), BF16),
            pltpu.VMEM((FR * BLK, HD), F32),
            pltpu.VMEM((HD, FR * BLK), BF16),
            pltpu.VMEM((FR * BLK, 2 * HD), BF16),
            pltpu.VMEM((FR * BLK, LAT), F32),
            pltpu.VMEM((BLK, LAT), F32),
            pltpu.VMEM((BLK, LAT), F32),
            pltpu.VMEM((FR, 32, LAT), BF16),
            pltpu.VMEM((NZ, 32, LAT), BF16),
            pltpu.VMEM((HD, LAT), BF16),
            pltpu.VMEM((FR, BLK, LAT), BF16),
            pltpu.VMEM((FR, BLK, LAT), BF16),
            pltpu.VMEM((8, 6, FR, LAT), BF16),
            pltpu.VMEM((6, 4, FR, CH), BF16),
            pltpu.VMEM((4 * 8 * FR, 9 * CH), BF16),
            dma((4,)),
            dma((1,)),
            dma((SUBS,)), dma((SUBS,)),
            dma((2,)), dma((2,)),
            dma((1,)), dma((1,)),
            dma((2, 4, SUBS)), dma((2, 4, SUBS)),
            dma((NZ, SUBS)), dma((NZ, SUBS)),
            dma((FR,)), dma((FR,)),
            dma((4,)), dma((4,)),
            dma((FR,)), dma((FR,)),
            dma((9,)), dma((9,)),
        ],
        compiler_params=pltpu.CompilerParams(
            collective_id=0, has_side_effects=True, vmem_limit_bytes=60 * 2**20
        ),
        cost_estimate=pl.CostEstimate(
            flops=13 * 10**9, bytes_accessed=14 * 10**6, transcendentals=5 * 10**6
        ),
    )(
        tokens[0],
        modulation,
        triple_weight.reshape(D, 3 * HD),
        out_weight.reshape(2, NZ, 4, 32, 256),
        gate.reshape(1, 256),
        latent_weight,
        conv_weight.reshape(3, 9 * LAT, CH),
        conv_bias.reshape(1, CH),
        res_weight.reshape(3, 9 * CH, CH),
        res_bias.reshape(1, CH),
    )
    out = out.reshape(2, 2, 4, 2, FR, CH)
    return out.transpose(4, 2, 0, 3, 1, 5).reshape(FR, 8, 4, CH)


def solution(mesh):
    placed = (
        P("grp", "tok", None),
        P(),
        P(None, None, "tok"),
        P(None, "tok"),
        P("tok"),
        P(),
        P(),
        P(),
        P(),
        P(),
    )
    return jax.shard_map(
        shards, mesh=mesh, in_specs=placed, out_specs=P(None, "grp", "tok", None), check_vma=False
    )
```

time: 454 us -> 137 us (0.30)
  waiting for transfers between devices: 327 us -> 0 us
  Pallas kernels: 0 us -> 129 us
  matrix products: 43.6 us -> 0 us
  starting transfers between devices: 25 us -> 0 us
  other arithmetic: 15.4 us -> 0 us
  between operations: 14 us -> 0.02 us
  blocking collectives: 13.2 us -> 0 us
  local copies, waits for them, and re-layouts: 13.2 us -> 8.07 us
    all_gather x2 -> x0, waiting for transfers between devices: 282 us -> none  [the longest x1 184 us: shards(): lax.all_gather(modulated, 'tok', axis=0, tiled=True)]
    pallas_call x0 -> x1, Pallas kernels: none -> 129 us  [shards(): pl.pallas_call(kernel, out_shape=jax.ShapeDtypeStruct((4, 4, 2, FR, CH),...]
    dot_general x8 -> x0, matrix products: 43.6 us -> none  [the longest x1 11.2 us: shards(): jnp.dot(lax.all_gather(modulated, 'tok', axis=0, tiled=True), local_weigh...]
    all_to_all x1 -> x0, waiting for transfers between devices: 23 us -> none  [shards(): lax.all_to_all(branch, 'tok', split_axis=0, concat_axis=1, tiled=True)]
    ppermute x8 -> x0, waiting for transfers between devices: 21.6 us -> none  [the longest x4 21 us: extended_2(): lax.ppermute(lax.slice_in_dim(block, 0, width, axis=dim), axis, backward)]
    ppermute x8 -> x0, starting transfers between devices: 20.6 us -> none  [the longest x4 14.2 us: extended_2(): lax.ppermute(lax.slice_in_dim(block, block.shape[dim] - width, None, axis...]
    all_to_all x1 -> x0, blocking collectives: 13.2 us -> none  [shards(): lax.all_to_all(latent, 'tok', split_axis=2, concat_axis=0, tiled=True)]
    reduce_sum x2 -> x0, other arithmetic: 10.2 us -> none  [the longest x1 8.55 us: shards(): jnp.sum(weights, axis=-1, keepdims=True)]
  transfers between devices with their start and end apart: 11 -> 0, of which waited for: 8 -> 0; matrix products, arithmetic and copies ran while one was open for 2% -> 0% of each run, Pallas kernels for 0% -> 0%
where the time goes in v1:
time: 137 us
  Pallas kernels  129 us (94%)
  local copies, waits for them, and re-layouts  8.07 us (6%)
    pallas_call x1, Pallas kernels, shards(): pl.pallas_call(kernel, out_shape=jax.ShapeDtypeStruct((4, 4, 2, FR, CH),...  129 us
    unnamed x1, local copies, waits for them, and re-layouts  3.19 us
    reshape x1, local copies, waits for them, and re-layouts, shards(): triple_weight.reshape(D, 3 * HD)  2.81 us

profile of v1, /device:TPU:7, one launch (start us, length us, event | category | flops | bytes accessed | tf_op | source)
XLA Modules:
  0.0 137.0 jit_solution(10410828880356314231)
XLA Ops:
  0.0 3.2 %copy.13 = bf16[4096,3,128]{0,2,1:T(8,128)(2,1)S(1)} copy(bf16[4096,3,128]{2,0,1:T(8,128)(2,1)} %param.12) | data formatting | bytes 6291456 | tf_op args[2]
  3.2 2.8 %copy.14.w_hbm = bf16[4096,384]{1,0:T(8,128)(2,1)} copy(bf16[4096,384]{0,1:T(8,128)(2,1)S(1)} %bitcast.11) | data formatting | bytes 6291456 | tf_op jit(solution)/shard_map/reshape | solution.py:612
  6.0 128.9 %shard_map.100 = bf16[4,4,2,16,256]{4,3,2,1,0:T(8,128)(2,1)} custom-call(bf16[128,4096]{1,0:T(8,128)(2,1)} %bitcast.15, f32[2,4096]{1,0:T(2,128)} %mod_ref.1, bf16[4096,384]{1,0:T(8,128)(2,1)} %copy.14.w_hbm, bf16[2,8,4,32,256]{4,3,2,1,0:T(8,128)(2,1)} %bitcast.16, f32[1,256]{1,0:T(1,128)} %bitcast.17, bf16[4096,128]{1,0:T(8,128)(2,1)} %lw_hbm.1, ...), custom_call_target="tpu_custom_call" | custom-call | flops 12999999488 | bytes 14000000 | tf_op jit(solution)/shard_map/pallas_call | solution.py:564
  134.9 1.2 copy.15
  136.1 0.8 reshape.35

commit v2 on v1

--- a/solution.py
+++ b/solution.py
@@ -20,7 +20,6 @@
 LAT = 128
 CH = 256
 NZ = 8
-W_CUT = 1408
 EXP_SCALE = HD ** (-0.5) * math.log2(math.e)
 
 
@@ -101,11 +100,17 @@
     load_rw = pltpu.make_async_copy(rw_hbm, rw, local_sem.at[3])
     load_lw.start()
     load_ow.start()
-    load_w = pltpu.make_async_copy(w_hbm, wv, wloc_sem.at[0])
+
+    def third(k):
+        return wv.at[:, pl.ds(k * HD, HD)]
+
+    def load_w(k):
+        return pltpu.make_async_copy(w_hbm.at[k], third(k), wloc_sem.at[k])
 
     @pl.when(jnp.logical_not(swapped))
     def _():
-        load_w.start()
+        for k in range(3):
+            load_w(k).start()
 
     load_cw.start()
     load_rw.start()
@@ -131,14 +136,13 @@
             xall.at[head, rows_of(sub)], xall.at[head, rows_of(sub)], swx_recv.at[sub]
         ).wait()
 
-    def swap_w(part):
-        rows = pl.ds(0, W_CUT) if part == 0 else pl.ds(W_CUT, D - W_CUT)
-        return pltpu.make_async_remote_copy(
-            src_ref=w_hbm.at[rows],
-            dst_ref=wv.at[rows],
-            send_sem=sww_send.at[part],
-            recv_sem=sww_recv.at[part],
-            device_id=(mate_grp if part == 0 else far_grp, mate_tok),
+    def swap_w(k):
+        return pltpu.make_async_remote_copy(
+            src_ref=w_hbm.at[k],
+            dst_ref=third(k),
+            send_sem=sww_send.at[k],
+            recv_sem=sww_recv.at[k],
+            device_id=(mate_grp if k == 2 else far_grp, mate_tok),
             device_id_type=MESH,
         )
 
@@ -214,6 +218,7 @@
     @pl.when(swapped)
     def _():
         swap_x(0).start()
+        swap_w(0).start()
         swap_w(1).start()
 
     @pl.when(jnp.logical_not(swapped))
@@ -227,7 +232,7 @@
     @pl.when(swapped)
     def _():
         swap_x(1).start()
-        swap_w(0).start()
+        swap_w(2).start()
         swap_r().start()
         wait_swap_x(0)
         ring(0, 0, 0).start()
@@ -324,13 +329,14 @@
 
     @pl.when(jnp.logical_not(swapped))
     def _():
-        load_w.wait()
+        for k in range(3):
+            load_w(k).wait()
         rbuf[...] = rmine[...]
 
     @pl.when(swapped)
     def _():
-        pltpu.make_async_copy(wv.at[pl.ds(W_CUT, D - W_CUT)], wv.at[pl.ds(W_CUT, D - W_CUT)], sww_recv.at[1]).wait()
-        pltpu.make_async_copy(wv.at[pl.ds(0, W_CUT)], wv.at[pl.ds(0, W_CUT)], sww_recv.at[0]).wait()
+        for k in range(3):
+            swap_w(k).wait_recv()
         pltpu.make_async_copy(rbuf, rbuf, swr_recv.at[0]).wait()
 
     def first(n, carry):
@@ -523,8 +529,8 @@
 
     @pl.when(swapped)
     def _():
-        swap_w(0).wait_send()
-        swap_w(1).wait_send()
+        for k in range(3):
+            swap_w(k).wait_send()
         swap_r().wait_send()
 
     lax.fori_loop(1, FR, fold_sent, 0)
@@ -589,9 +595,9 @@
             pltpu.VMEM((6, 4, FR, CH), BF16),
             pltpu.VMEM((4 * 8 * FR, 9 * CH), BF16),
             dma((4,)),
-            dma((1,)),
+            dma((3,)),
             dma((SUBS,)), dma((SUBS,)),
-            dma((2,)), dma((2,)),
+            dma((3,)), dma((3,)),
             dma((1,)), dma((1,)),
             dma((2, 4, SUBS)), dma((2, 4, SUBS)),
             dma((NZ, SUBS)), dma((NZ, SUBS)),
@@ -609,7 +615,7 @@
     )(
         tokens[0],
         modulation,
-        triple_weight.reshape(D, 3 * HD),
+        triple_weight.transpose(1, 0, 2),
         out_weight.reshape(2, NZ, 4, 32, 256),
         gate.reshape(1, 256),
         latent_weight,

time: 137 us -> 131 us (0.956)
  local copies, waits for them, and re-layouts: 8.07 us -> 2.07 us
    unnamed x1 -> x0, local copies, waits for them, and re-layouts: 3.19 us -> none
    reshape x1 -> x0, local copies, waits for them, and re-layouts: 2.81 us -> none  [shards(): triple_weight.reshape(D, 3 * HD)]
where the time goes in v2:
time: 131 us
  Pallas kernels  129 us (98%)
  local copies, waits for them, and re-layouts  2.07 us (2%)
    pallas_call x1, Pallas kernels, shards(): pl.pallas_call(kernel, out_shape=jax.ShapeDtypeStruct((4, 4, 2, FR, CH),...  129 us

profile of v2, /device:TPU:7, one launch (start us, length us, event | category | flops | bytes accessed | tf_op | source)
XLA Modules:
  0.0 130.9 jit_solution(14252542621693134451)
XLA Ops:
  0.0 128.9 %shard_map.100 = bf16[4,4,2,16,256]{4,3,2,1,0:T(8,128)(2,1)} custom-call(bf16[128,4096]{1,0:T(8,128)(2,1)} %bitcast.15, f32[2,4096]{1,0:T(2,128)} %mod_ref.1, bf16[3,4096,128]{2,1,0:T(8,128)(2,1)} %bitcast.13, bf16[2,8,4,32,256]{4,3,2,1,0:T(8,128)(2,1)} %bitcast.16, f32[1,256]{1,0:T(1,128)} %bitcast.17, bf16[4096,128]{1,0:T(8,128)(2,1)} %lw_hbm.1, ...), custom_call_target="tpu_custom_call" | custom-call | flops 12999999488 | bytes 14000000 | tf_op jit(solution)/shard_map/pallas_call | solution.py:570
  128.9 1.2 copy.11
  130.1 0.8 reshape.31

commit v3 on v2

--- a/solution.py
+++ b/solution.py
@@ -15,11 +15,12 @@
 HD = 128
 FR = 16
 BLK = 128
-SUBS = 2
+SUBS = 4
 SUB = BLK // SUBS
 LAT = 128
 CH = 256
 NZ = 8
+EARLY = 14 * BLK
 EXP_SCALE = HD ** (-0.5) * math.log2(math.e)
 
 
@@ -27,10 +28,10 @@
     tok_ref, mod_ref, w_hbm, ow_hbm, gate_ref, lw_hbm, cw_hbm, cb_ref, rw_hbm, rb_ref,
     out_ref,
     xall, xown, wv, lw, ow, cw, rw, qs, kt, v2, radd, rmine, rbuf, mrecv, msend, mfull,
-    lsend, lrecv, ext, coarse, cols2,
+    lsend, lrecv, psend, precv, pmine, tops, sums, weights, order, ext, coarse, cols2,
     local_sem, wloc_sem, swx_send, swx_recv, sww_send, sww_recv, swr_send, swr_recv,
     ring_send, ring_recv, sib_send, sib_recv, m_send, m_recv, mx_send, mx_recv,
-    l_send, l_recv, h_send, h_recv,
+    l_send, l_recv, p_send, p_recv, h_send, h_recv,
 ):
     g = lax.axis_index("grp")
     t = lax.axis_index("tok")
@@ -115,9 +116,6 @@
     load_cw.start()
     load_rw.start()
 
-    v2[:, HD:] = jnp.ones((v2.shape[0], HD), BF16)
-    radd[...] = jnp.zeros_like(radd)
-
     def rows_of(sub):
         return pl.ds(sub * SUB, SUB)
 
@@ -189,8 +187,6 @@
 
     reach = (4 - core, 3 + core)
 
-    load_lw.wait()
-
     new = lax.broadcasted_iota(jnp.int32, (BLK, BLK), 0)
     old = lax.broadcasted_iota(jnp.int32, (BLK, BLK), 1)
     source = (lax.rem(new // 2, 4)) * 32 + (new // 8) * 2 + lax.rem(new, 2)
@@ -200,7 +196,6 @@
         own = jnp.dot(
             pick[sub * SUB : (sub + 1) * SUB], tok_ref[...], preferred_element_type=F32
         )
-        rmine[rows_of(sub), :] = jnp.dot(own.astype(BF16), lw[...], preferred_element_type=F32)
         scale = lax.rsqrt(jnp.mean(own * own, axis=-1, keepdims=True) + 1e-06)
         made = (own * scale * (1.0 + mod_ref[1:2, :]) + mod_ref[0:1, :]).astype(BF16)
 
@@ -212,37 +207,48 @@
         def _():
             xall[head, rows_of(sub), :] = made
 
-    prepare(0)
-    pl.semaphore_wait(barrier, guests)
+    def depart(sub):
+        ring(0, 0, sub).start()
+        ring(1, 0, sub).start()
+        share(z, sub).start()
+
+    for sub in range(SUBS):
+        prepare(sub)
+        if sub == 0:
+            pl.semaphore_wait(barrier, guests)
+
+        @pl.when(swapped)
+        def _():
+            swap_x(sub).start()
+            if sub < 2:
+                swap_w(sub).start()
+
+        @pl.when(jnp.logical_not(swapped))
+        def _():
+            depart(sub)
+
+    load_lw.wait()
+    own_rows = jnp.dot(pick, tok_ref[...], preferred_element_type=F32).astype(BF16)
+    rmine[...] = jnp.dot(own_rows, lw[...], preferred_element_type=F32)
 
     @pl.when(swapped)
     def _():
-        swap_x(0).start()
-        swap_w(0).start()
-        swap_w(1).start()
-
-    @pl.when(jnp.logical_not(swapped))
-    def _():
-        ring(0, 0, 0).start()
-        ring(1, 0, 0).start()
-        share(z, 0).start()
-
-    prepare(1)
-
-    @pl.when(swapped)
-    def _():
-        swap_x(1).start()
         swap_w(2).start()
         swap_r().start()
-        wait_swap_x(0)
-        ring(0, 0, 0).start()
-        ring(1, 0, 0).start()
-        share(z, 0).start()
-        wait_swap_x(1)
-
-    ring(0, 0, 1).start()
-    ring(1, 0, 1).start()
-    share(z, 1).start()
+        for sub in range(SUBS):
+            wait_swap_x(sub)
+            depart(sub)
+
+    v2[:, HD:] = jnp.ones((v2.shape[0], HD), BF16)
+    radd[...] = jnp.zeros_like(radd)
+    qs[...] = jnp.zeros_like(qs)
+    to = lax.broadcasted_iota(jnp.int32, (4 * BLK, 4 * BLK), 0)
+    of = lax.broadcasted_iota(jnp.int32, (4 * BLK, 4 * BLK), 1)
+    row, col = lax.rem(to // 4, 8), lax.rem(to, 4)
+    phase = lax.rem(row, 2) * 2 + lax.rem(col, 2)
+    order[...] = jnp.where(
+        of == phase * BLK + (row // 2) * 32 + (col // 2) * FR + to // 32, 1.0, 0.0
+    ).astype(BF16)
 
     load_ow.wait()
     scaled = (ow[...].astype(F32) * gate_ref[...]).astype(BF16).reshape(NZ * 32, 256)
@@ -294,7 +300,8 @@
         slot = kind * NZ + origin
         triple = jnp.dot(xall[slot], wv[...], preferred_element_type=F32)
         qs[pl.ds(slot, BLK, stride=FR), :] = triple[:, :HD]
-        at = pl.ds(pl.multiple_of(slot * BLK, BLK), BLK)
+        place = 2 * lax.rem(origin - z + NZ + 3, NZ) + jnp.where(kind == core, 0, 1)
+        at = pl.ds(pl.multiple_of(place * BLK, BLK), BLK)
         kt[:, at] = triple[:, HD : 2 * HD].T.astype(BF16)
         v2[at, :HD] = triple[:, 2 * HD :].astype(BF16)
 
@@ -364,62 +371,119 @@
     for step in range(1, 4):
         there = lax.rem(x + step, n_x)
         pltpu.make_async_copy(fold_rows(there), fold_rows(there), mx_recv.at[there]).wait()
+
+    def early(query):
+        scores = jnp.dot(query.astype(BF16), kt[:, :EARLY], preferred_element_type=F32)
+        top = jnp.max(scores, axis=-1, keepdims=True)
+        probs = jnp.exp2((scores - top) * EXP_SCALE).astype(BF16)
+        return top, jnp.dot(probs, v2[:EARLY, :], preferred_element_type=F32)
+
+    def attend_early(n, carry):
+        at = pl.ds(pl.multiple_of(n * 256, 256), 256)
+        top, summed = early(qs[at, :])
+        tops[at, :] = jnp.broadcast_to(top, (256, HD))
+        sums[at, :] = summed[:, :HD]
+        weights[at, :] = summed[:, HD:]
+        return carry
+
+    lax.fori_loop(0, FR // 2, attend_early, 0)
     forward(4)
     last = lax.rem(z + 4, NZ)
     project(core, last)
     project_sib(last)
 
+    late_rows = [pl.ds(kind * NZ + last, BLK, stride=FR) for kind in range(2)]
+    top, summed = early(jnp.concatenate([qs[rows, :] for rows in late_rows], axis=0))
+    for kind in range(2):
+        piece = slice(kind * BLK, (kind + 1) * BLK)
+        tops[late_rows[kind], :] = jnp.broadcast_to(top[piece], (BLK, HD))
+        sums[late_rows[kind], :] = summed[piece, :HD]
+        weights[late_rows[kind], :] = summed[piece, HD:]
+
     home = pair + y_lo
 
-    def latent_copy(target):
-        return pltpu.make_async_remote_copy(
-            src_ref=lsend.at[target],
-            dst_ref=lrecv.at[head],
-            send_sem=l_send.at[target],
-            recv_sem=l_recv.at[head],
-            device_id=(home, target),
-            device_id_type=MESH,
-        )
-
-    def is_self(target):
-        return jnp.logical_and(home == g, target == t)
-
-    def attend(n, carry):
-        two = lax.rem(n + t // 2 + 1, FR // 2)
+    def latent_copy(two):
+        return pltpu.make_async_remote_copy(
+            src_ref=lsend.at[two],
+            dst_ref=lrecv.at[z],
+            send_sem=l_send.at[two],
+            recv_sem=l_recv.at[z],
+            device_id=(home, two * 2 + core),
+            device_id_type=MESH,
+        )
+
+    def to_sibling(two):
+        return pltpu.make_async_remote_copy(
+            src_ref=psend.at[two],
+            dst_ref=precv.at[two],
+            send_sem=p_send.at[two],
+            recv_sem=p_recv.at[two],
+            device_id=(sib_grp, t),
+            device_id_type=MESH,
+        )
+
+    def is_self(two):
+        return jnp.logical_and(home == g, two * 2 + core == t)
+
+    def turn(n):
+        return lax.rem(n + t // 2 + 1, FR // 2)
+
+    def attend(n):
+        two = turn(n)
         at = pl.ds(pl.multiple_of(two * 256, 256), 256)
-        scores = jnp.dot(qs[at, :].astype(BF16), kt[...], preferred_element_type=F32)
-        top = jnp.max(scores, axis=-1, keepdims=True)
-        probs = jnp.exp2((scores - top) * EXP_SCALE).astype(BF16)
-        summed = jnp.dot(probs, v2[...], preferred_element_type=F32)
-        attended = (summed[:, :HD] / summed[:, HD:]).astype(BF16)
+        scores = jnp.dot(qs[at, :].astype(BF16), kt[:, EARLY:], preferred_element_type=F32)
+        before = tops[at, :]
+        top = jnp.maximum(before, jnp.max(scores, axis=-1, keepdims=True))
+        shrink = jnp.exp2((before - top) * EXP_SCALE)
+        both_tops = jnp.concatenate([top, top], axis=1)
+        probs = jnp.exp2((scores - both_tops) * EXP_SCALE).astype(BF16)
+        summed = jnp.dot(probs, v2[EARLY:, :], preferred_element_type=F32)
+        values = sums[at, :] * shrink + summed[:, :HD]
+        weight = weights[at, :] * shrink + summed[:, HD:]
+        attended = (values / weight).astype(BF16)
         latent = jnp.dot(attended, mfull[...], preferred_element_type=F32) + radd[at, :]
-        pieces = latent.astype(BF16).reshape(2, BLK, LAT)
-        lsend[pl.ds(pl.multiple_of(two * 2, 2), 2)] = pieces
-        for half in range(2):
-            target = two * 2 + half
-
-            @pl.when(jnp.logical_not(is_self(target)))
-            def _():
-                latent_copy(target).start()
-
-            @pl.when(is_self(target))
-            def _():
-                lrecv[head] = pieces[half]
-
-        return carry
-
-    lax.fori_loop(0, FR // 2, attend, 0)
+        mine = jnp.where(core == 0, latent[:BLK], latent[BLK:])
+        other = jnp.where(core == 0, latent[BLK:], latent[:BLK])
+        psend[two] = other.astype(BF16)
+        to_sibling(two).start()
+        pmine[two] = mine
+
+    def pass_on(n):
+        two = turn(n)
+        to_sibling(two).wait_recv()
+        summed = (pmine[two] + precv[two].astype(F32)).astype(BF16)
+
+        @pl.when(jnp.logical_not(is_self(two)))
+        def _():
+            lsend[two] = summed
+            latent_copy(two).start()
+
+        @pl.when(is_self(two))
+        def _():
+            lrecv[z] = summed
+
+    attend(0)
+
+    def attend_and_pass(n, carry):
+        attend(n)
+        pass_on(n - 1)
+        return carry
+
+    lax.fori_loop(1, FR // 2, attend_and_pass, 0)
+    pass_on(FR // 2 - 1)
 
     def latent_wait(n, carry):
-        @pl.when(jnp.logical_not(jnp.logical_and(core == y_lo, n == head)))
+        here = jnp.logical_and(core == y_lo, lax.rem(t, 2) == core)
+
+        @pl.when(jnp.logical_not(jnp.logical_and(here, n == z)))
         def _():
             pltpu.make_async_copy(lrecv.at[n], lrecv.at[n], l_recv.at[n]).wait()
 
         return carry
 
-    lax.fori_loop(0, FR, latent_wait, 0)
+    lax.fori_loop(0, NZ, latent_wait, 0)
     tile = lrecv[0].astype(F32)
-    for n in range(1, FR):
+    for n in range(1, NZ):
         tile = tile + lrecv[n].astype(F32)
     ext[2:6, 2:4] = tile.astype(BF16).reshape(4, 2, FR, LAT)
 
@@ -507,9 +571,9 @@
     three = [jnp.dot(cols2[...], rw[a], preferred_element_type=F32) for a in range(3)]
     mixed = over_frames(three, 4 * rows)
     center = coarse[1:5, 1:3].reshape(rows, CH).astype(F32)
-    for n in range(4):
-        result = silu(center + mixed[n * rows : (n + 1) * rows] + rb_ref[...])
-        out_ref[n] = result.astype(BF16).reshape(4, 2, FR, CH)
+    center = jnp.concatenate([center] * 4, axis=0)
+    result = silu(center + mixed + rb_ref[...]).astype(BF16)
+    out_ref[...] = jnp.dot(order[...], result, preferred_element_type=F32).astype(BF16)
 
     for sub in range(SUBS):
 
@@ -537,14 +601,16 @@
     for step in range(1, 4):
         spread(step).wait_send()
 
-    def latent_sent(target, carry):
-        @pl.when(jnp.logical_not(is_self(target)))
-        def _():
-            latent_copy(target).wait_send()
-
-        return carry
-
-    lax.fori_loop(0, FR, latent_sent, 0)
+    def latent_sent(two, carry):
+        to_sibling(two).wait_send()
+
+        @pl.when(jnp.logical_not(is_self(two)))
+        def _():
+            latent_copy(two).wait_send()
+
+        return carry
+
+    lax.fori_loop(0, FR // 2, latent_sent, 0)
     for dg, dt in ways:
 
         @pl.when(inside(dg, dt))
@@ -569,7 +635,7 @@
     dma = pltpu.SemaphoreType.DMA
     out = pl.pallas_call(
         kernel,
-        out_shape=jax.ShapeDtypeStruct((4, 4, 2, FR, CH), BF16),
+        out_shape=jax.ShapeDtypeStruct((4 * BLK, CH), BF16),
         in_specs=[vmem, vmem, hbm, hbm, vmem, hbm, hbm, vmem, hbm, vmem],
         out_specs=vmem,
         scratch_shapes=[
@@ -589,8 +655,15 @@
             pltpu.VMEM((FR, 32, LAT), BF16),
             pltpu.VMEM((NZ, 32, LAT), BF16),
             pltpu.VMEM((HD, LAT), BF16),
-            pltpu.VMEM((FR, BLK, LAT), BF16),
-            pltpu.VMEM((FR, BLK, LAT), BF16),
+            pltpu.VMEM((NZ, BLK, LAT), BF16),
+            pltpu.VMEM((NZ, BLK, LAT), BF16),
+            pltpu.VMEM((NZ, BLK, LAT), BF16),
+            pltpu.VMEM((NZ, BLK, LAT), BF16),
+            pltpu.VMEM((NZ, BLK, LAT), F32),
+            pltpu.VMEM((FR * BLK, HD), F32),
+            pltpu.VMEM((FR * BLK, HD), F32),
+            pltpu.VMEM((FR * BLK, HD), F32),
+            pltpu.VMEM((4 * BLK, 4 * BLK), BF16),
             pltpu.VMEM((8, 6, FR, LAT), BF16),
             pltpu.VMEM((6, 4, FR, CH), BF16),
             pltpu.VMEM((4 * 8 * FR, 9 * CH), BF16),
@@ -603,7 +676,8 @@
             dma((NZ, SUBS)), dma((NZ, SUBS)),
             dma((FR,)), dma((FR,)),
             dma((4,)), dma((4,)),
-            dma((FR,)), dma((FR,)),
+            dma((NZ,)), dma((NZ,)),
+            dma((NZ,)), dma((NZ,)),
             dma((9,)), dma((9,)),
         ],
         compiler_params=pltpu.CompilerParams(
@@ -624,8 +698,7 @@
         res_weight.reshape(3, 9 * CH, CH),
         res_bias.reshape(1, CH),
     )
-    out = out.reshape(2, 2, 4, 2, FR, CH)
-    return out.transpose(4, 2, 0, 3, 1, 5).reshape(FR, 8, 4, CH)
+    return out.reshape(FR, 8, 4, CH)
 
 
 def solution(mesh):

time: 131 us -> 131 us (level)
  no operation moved by 1% of the time
where the time goes in v3:
time: 131 us
  Pallas kernels  129 us (98%)
  local copies, waits for them, and re-layouts  1.72 us (1%)
    pallas_call x1, Pallas kernels, shards(): pl.pallas_call(kernel, out_shape=jax.ShapeDtypeStruct((4 * BLK, CH), BF16...  129 us

profile of v3, /device:TPU:7, one launch (start us, length us, event | category | flops | bytes accessed | tf_op | source)
XLA Modules:
  0.0 131.2 jit_solution(513403635482031611)
XLA Ops:
  0.0 129.4 %shard_map.100 = bf16[512,256]{1,0:T(8,128)(2,1)} custom-call(bf16[128,4096]{1,0:T(8,128)(2,1)} %bitcast.11, f32[2,4096]{1,0:T(2,128)} %mod_ref.1, bf16[3,4096,128]{2,1,0:T(8,128)(2,1)} %bitcast.9, bf16[2,8,4,32,256]{4,3,2,1,0:T(8,128)(2,1)} %bitcast.12, f32[1,256]{1,0:T(1,128)} %bitcast.13, bf16[4096,128]{1,0:T(8,128)(2,1)} %lw_hbm.1, ...), custom_call_target="tpu_custom_call" | custom-call | flops 12999999488 | bytes 14000000 | tf_op jit(solution)/shard_map/pallas_call | solution.py:636
  129.4 1.7 %reshape.27 = bf16[16,8,4,256]{3,2,1,0:T(4,128)(2,1)} reshape(bf16[512,256]{1,0:T(8,128)(2,1)} %shard_map.100) | data formatting | bytes 524288 | tf_op jit(solution)/shard_map/reshape | solution.py:701

commit v4 on v3

--- a/solution.py
+++ b/solution.py
@@ -20,15 +20,14 @@
 LAT = 128
 CH = 256
 NZ = 8
-EARLY = 14 * BLK
 EXP_SCALE = HD ** (-0.5) * math.log2(math.e)
 
 
 def kernel(
     tok_ref, mod_ref, w_hbm, ow_hbm, gate_ref, lw_hbm, cw_hbm, cb_ref, rw_hbm, rb_ref,
     out_ref,
-    xall, xown, wv, lw, ow, cw, rw, qs, kt, v2, radd, rmine, rbuf, mrecv, msend, mfull,
-    lsend, lrecv, psend, precv, pmine, tops, sums, weights, order, ext, coarse, cols2,
+    xall, xown, wv, lw, ow, cw, rw, qs, kt, v2, rmine, rbuf, mrecv, msend, mfull,
+    lsend, lrecv, psend, precv, lat, tops, sums, order, ext, coarse, cols2,
     local_sem, wloc_sem, swx_send, swx_recv, sww_send, sww_recv, swr_send, swr_recv,
     ring_send, ring_recv, sib_send, sib_recv, m_send, m_recv, mx_send, mx_recv,
     l_send, l_recv, p_send, p_recv, h_send, h_recv,
@@ -239,9 +238,126 @@
             wait_swap_x(sub)
             depart(sub)
 
+    def fold_copy(other):
+        return pltpu.make_async_remote_copy(
+            src_ref=msend.at[lax.rem(other, NZ)],
+            dst_ref=mrecv.at[t],
+            send_sem=m_send.at[other],
+            recv_sem=m_recv.at[t],
+            device_id=(g, other),
+            device_id_type=MESH,
+        )
+
+    def fold_wait(step, carry):
+        other = lax.rem(t + step, FR)
+        pltpu.make_async_copy(mrecv.at[other], mrecv.at[other], m_recv.at[other]).wait()
+        return carry
+
+    def fold_sent(step, carry):
+        fold_copy(lax.rem(t + step, FR)).wait_send()
+        return carry
+
+    def fold_rows(which):
+        return mfull.at[pl.ds(pl.multiple_of(which * 32, 32), 32)]
+
+    def spread(step):
+        return pltpu.make_async_remote_copy(
+            src_ref=fold_rows(x),
+            dst_ref=fold_rows(x),
+            send_sem=mx_send.at[step],
+            recv_sem=mx_recv.at[x],
+            device_id=(y_hi * (2 * n_x) + lax.rem(x + step, n_x) * 2 + core, t),
+            device_id_type=MESH,
+        )
+
+    def place_of(p):
+        if isinstance(p, int):
+            table = [(k, o) for k in (0, 1) for o in (0, 1, -1)]
+            for far in (2, 3):
+                table += [(k, o) for k in (0, 1) for o in (far, -far)]
+            return (table + [(0, 4), (1, 4)])[p]
+        stage, p = p
+        if stage == 0:
+            return p // 3, lax.rem(p + 1, 3) - 1
+        if stage < 3:
+            return (p - 4 * stage - 2) // 2, (stage + 1) * (1 - 2 * lax.rem(p, 2))
+        return p - 14, 4
+
+    def slot_of(p):
+        kind, offset = place_of(p)
+        return jnp.where(kind == 0, core, 1 - core) * NZ + lax.rem(z + NZ + offset, NZ)
+
+    def project(stage, low, high):
+        def one(p, carry):
+            kind, offset = place_of((stage, p))
+            origin = lax.rem(z + NZ + offset, NZ)
+
+            @pl.when(kind == 1)
+            def _():
+                for sub in range(SUBS):
+                    block = xall.at[(1 - core) * NZ + origin, rows_of(sub)]
+                    pltpu.make_async_copy(block, block, sib_recv.at[origin, sub]).wait()
+
+            triple = jnp.dot(xall[slot_of((stage, p))], wv[...], preferred_element_type=F32)
+            qs[p] = (triple[:, :HD] * EXP_SCALE).astype(BF16)
+            at = pl.ds(pl.multiple_of(p * BLK, BLK), BLK)
+            kt[:, at] = triple[:, HD : 2 * HD].T.astype(BF16)
+            v2[at, :HD] = triple[:, 2 * HD :].astype(BF16)
+            return carry
+
+        lax.fori_loop(low, high, one, 0)
+
+    def forward(step, sub):
+        for way in range(2):
+
+            @pl.when(step <= reach[way])
+            def _():
+                wait_ring(way, step, sub)
+
+                @pl.when(step < reach[way])
+                def _():
+                    ring(way, step, sub).start()
+
+                share(origin_of(way, step), sub).start()
+
+    def meet(query, low, high, before=None):
+        keys = slice(low * BLK, high * BLK)
+        scores = jnp.dot(query, kt[:, keys], preferred_element_type=F32)
+        top = jnp.max(scores, axis=-1, keepdims=True)
+        top = jnp.broadcast_to(top, (query.shape[0], HD))
+        if before is not None:
+            top = jnp.maximum(before, top)
+        probs = jnp.exp2(scores - jnp.concatenate([top] * (high - low), axis=1))
+        return top, jnp.dot(probs.astype(BF16), v2[keys, :], preferred_element_type=F32)
+
+    def merged(summed, before, top, added):
+        shrink = jnp.exp2(before - top)
+        return summed * jnp.concatenate([shrink, shrink], axis=1) + added
+
+    def fresh(low, high, upto):
+        def one(n, carry):
+            at = pl.ds(2 * n, 2)
+            top, summed = meet(qs[at].reshape(2 * BLK, HD), 0, upto)
+            tops[at] = top.reshape(2, BLK, HD)
+            sums[at] = summed.reshape(2, BLK, 2 * HD)
+            return carry
+
+        lax.fori_loop(low // 2, high // 2, one, 0)
+
+    def update(rows, low, high):
+        def one(n, carry):
+            at = pl.ds(2 * n, 2)
+            before = tops[at].reshape(2 * BLK, HD)
+            top, added = meet(qs[at].reshape(2 * BLK, HD), low, high, before)
+            summed = merged(sums[at].reshape(2 * BLK, 2 * HD), before, top, added)
+            tops[at] = top.reshape(2, BLK, HD)
+            sums[at] = summed.reshape(2, BLK, 2 * HD)
+            return carry
+
+        lax.fori_loop(0, rows // 2, one, 0)
+
+    forward(1, 0)
     v2[:, HD:] = jnp.ones((v2.shape[0], HD), BF16)
-    radd[...] = jnp.zeros_like(radd)
-    qs[...] = jnp.zeros_like(qs)
     to = lax.broadcasted_iota(jnp.int32, (4 * BLK, 4 * BLK), 0)
     of = lax.broadcasted_iota(jnp.int32, (4 * BLK, 4 * BLK), 1)
     row, col = lax.rem(to // 4, 8), lax.rem(to, 4)
@@ -250,22 +366,13 @@
         of == phase * BLK + (row // 2) * 32 + (col // 2) * FR + to // 32, 1.0, 0.0
     ).astype(BF16)
 
+    forward(1, 1)
     load_ow.wait()
     scaled = (ow[...].astype(F32) * gate_ref[...]).astype(BF16).reshape(NZ * 32, 256)
     cols = pl.ds(pl.multiple_of(t * 256, 256), 256)
     part = jnp.dot(scaled, lw[cols, :], preferred_element_type=F32)
     msend[...] = part.astype(BF16).reshape(NZ, 32, LAT)
 
-    def fold_copy(other):
-        return pltpu.make_async_remote_copy(
-            src_ref=msend.at[lax.rem(other, NZ)],
-            dst_ref=mrecv.at[t],
-            send_sem=m_send.at[other],
-            recv_sem=m_recv.at[t],
-            device_id=(g, other),
-            device_id_type=MESH,
-        )
-
     mrecv[t] = msend[z]
 
     def fold_send(step, carry):
@@ -274,65 +381,9 @@
 
     lax.fori_loop(1, FR, fold_send, 0)
 
-    def fold_wait(step, carry):
-        other = lax.rem(t + step, FR)
-        pltpu.make_async_copy(mrecv.at[other], mrecv.at[other], m_recv.at[other]).wait()
-        return carry
-
-    def fold_sent(step, carry):
-        fold_copy(lax.rem(t + step, FR)).wait_send()
-        return carry
-
-    def fold_rows(which):
-        return mfull.at[pl.ds(pl.multiple_of(which * 32, 32), 32)]
-
-    def spread(step):
-        return pltpu.make_async_remote_copy(
-            src_ref=fold_rows(x),
-            dst_ref=fold_rows(x),
-            send_sem=mx_send.at[step],
-            recv_sem=mx_recv.at[x],
-            device_id=(y_hi * (2 * n_x) + lax.rem(x + step, n_x) * 2 + core, t),
-            device_id_type=MESH,
-        )
-
-    def project(kind, origin):
-        slot = kind * NZ + origin
-        triple = jnp.dot(xall[slot], wv[...], preferred_element_type=F32)
-        qs[pl.ds(slot, BLK, stride=FR), :] = triple[:, :HD]
-        place = 2 * lax.rem(origin - z + NZ + 3, NZ) + jnp.where(kind == core, 0, 1)
-        at = pl.ds(pl.multiple_of(place * BLK, BLK), BLK)
-        kt[:, at] = triple[:, HD : 2 * HD].T.astype(BF16)
-        v2[at, :HD] = triple[:, 2 * HD :].astype(BF16)
-
-    def project_sib(origin):
-        for sub in range(SUBS):
-            block = xall.at[(1 - core) * NZ + origin, rows_of(sub)]
-            pltpu.make_async_copy(block, block, sib_recv.at[origin, sub]).wait()
-        project(1 - core, origin)
-
-    def forward(step):
-        for sub in range(SUBS):
-            for way in range(2):
-
-                @pl.when(step <= reach[way])
-                def _():
-                    wait_ring(way, step, sub)
-
-                    @pl.when(step < reach[way])
-                    def _():
-                        ring(way, step, sub).start()
-
-                    share(origin_of(way, step), sub).start()
-
-    def both(step, work):
-        def go(way, carry):
-            work(lax.rem(z + NZ + (2 * way - 1) * step, NZ))
-            return carry
-
-        lax.fori_loop(0, 2, go, 0)
-
-    forward(1)
+    forward(1, 2)
+    forward(1, 3)
+    forward(2, 0)
 
     @pl.when(jnp.logical_not(swapped))
     def _():
@@ -346,13 +397,16 @@
             swap_w(k).wait_recv()
         pltpu.make_async_copy(rbuf, rbuf, swr_recv.at[0]).wait()
 
-    def first(n, carry):
-        project(core, lax.rem(z + NZ + lax.rem(n + 1, 3) - 1, NZ))
-        return carry
-
-    lax.fori_loop(0, 3, first, 0)
-    project_sib(z)
-    radd[pl.ds(head, BLK, stride=FR), :] = rbuf[...]
+    project(0, 0, 2)
+    forward(2, 1)
+    project(0, 2, 4)
+    forward(2, 2)
+    project(0, 4, 6)
+    forward(2, 3)
+    fresh(0, 6, 6)
+
+    forward(3, 0)
+    project(1, 6, 8)
     lax.fori_loop(1, FR, fold_wait, 0)
     total = mrecv[0].astype(F32)
     for other in range(1, FR):
@@ -360,45 +414,25 @@
     mfull[pl.ds(pl.multiple_of(x * 32, 32), 32), :] = total.astype(BF16)
     for step in range(1, 4):
         spread(step).start()
-
-    forward(2)
-    both(2, lambda origin: project(core, origin))
-    both(1, project_sib)
-    forward(3)
-    both(3, lambda origin: project(core, origin))
-    both(2, project_sib)
-    both(3, project_sib)
+    forward(3, 1)
+    project(1, 8, 10)
+    forward(3, 2)
+    update(6, 6, 10)
+    forward(3, 3)
+    fresh(6, 10, 10)
+
+    forward(4, 0)
+    project(2, 10, 12)
+    forward(4, 1)
+    project(2, 12, 14)
+    forward(4, 2)
+    update(10, 10, 14)
+    fresh(10, 14, 14)
     for step in range(1, 4):
         there = lax.rem(x + step, n_x)
         pltpu.make_async_copy(fold_rows(there), fold_rows(there), mx_recv.at[there]).wait()
-
-    def early(query):
-        scores = jnp.dot(query.astype(BF16), kt[:, :EARLY], preferred_element_type=F32)
-        top = jnp.max(scores, axis=-1, keepdims=True)
-        probs = jnp.exp2((scores - top) * EXP_SCALE).astype(BF16)
-        return top, jnp.dot(probs, v2[:EARLY, :], preferred_element_type=F32)
-
-    def attend_early(n, carry):
-        at = pl.ds(pl.multiple_of(n * 256, 256), 256)
-        top, summed = early(qs[at, :])
-        tops[at, :] = jnp.broadcast_to(top, (256, HD))
-        sums[at, :] = summed[:, :HD]
-        weights[at, :] = summed[:, HD:]
-        return carry
-
-    lax.fori_loop(0, FR // 2, attend_early, 0)
-    forward(4)
-    last = lax.rem(z + 4, NZ)
-    project(core, last)
-    project_sib(last)
-
-    late_rows = [pl.ds(kind * NZ + last, BLK, stride=FR) for kind in range(2)]
-    top, summed = early(jnp.concatenate([qs[rows, :] for rows in late_rows], axis=0))
-    for kind in range(2):
-        piece = slice(kind * BLK, (kind + 1) * BLK)
-        tops[late_rows[kind], :] = jnp.broadcast_to(top[piece], (BLK, HD))
-        sums[late_rows[kind], :] = summed[piece, :HD]
-        weights[late_rows[kind], :] = summed[piece, HD:]
+    forward(4, 3)
+    project(3, 14, 16)
 
     home = pair + y_lo
 
@@ -425,33 +459,35 @@
     def is_self(two):
         return jnp.logical_and(home == g, two * 2 + core == t)
 
-    def turn(n):
-        return lax.rem(n + t // 2 + 1, FR // 2)
-
-    def attend(n):
-        two = turn(n)
-        at = pl.ds(pl.multiple_of(two * 256, 256), 256)
-        scores = jnp.dot(qs[at, :].astype(BF16), kt[:, EARLY:], preferred_element_type=F32)
-        before = tops[at, :]
-        top = jnp.maximum(before, jnp.max(scores, axis=-1, keepdims=True))
-        shrink = jnp.exp2((before - top) * EXP_SCALE)
-        both_tops = jnp.concatenate([top, top], axis=1)
-        probs = jnp.exp2((scores - both_tops) * EXP_SCALE).astype(BF16)
-        summed = jnp.dot(probs, v2[EARLY:, :], preferred_element_type=F32)
-        values = sums[at, :] * shrink + summed[:, :HD]
-        weight = weights[at, :] * shrink + summed[:, HD:]
-        attended = (values / weight).astype(BF16)
-        latent = jnp.dot(attended, mfull[...], preferred_element_type=F32) + radd[at, :]
-        mine = jnp.where(core == 0, latent[:BLK], latent[BLK:])
-        other = jnp.where(core == 0, latent[BLK:], latent[:BLK])
-        psend[two] = other.astype(BF16)
-        to_sibling(two).start()
-        pmine[two] = mine
-
-    def pass_on(n):
-        two = turn(n)
+    def half_of(two, which):
+        return lat[pl.ds(pl.multiple_of(two * 256 + which * BLK, BLK), BLK), :]
+
+    H = BLK // 2
+
+    def finish(half):
+        part = pl.ds(half * H, H)
+        before = tops[0:14, part].reshape(14 * H, HD)
+        top, added = meet(qs[0:14, part].reshape(14 * H, HD), 14, 16, before)
+        older = merged(sums[0:14, part].reshape(14 * H, 2 * HD), before, top, added)
+        newer = meet(qs[14:16, part].reshape(2 * H, HD), 0, 16)[1]
+        summed = jnp.concatenate([older, newer], axis=0)
+        attended = (summed[:, :HD] / summed[:, HD:]).astype(BF16)
+        latent = jnp.dot(attended, mfull[...], preferred_element_type=F32)
+        for p in range(16):
+            piece = latent[p * H : (p + 1) * H]
+            if p == 0:
+                piece = piece + rbuf[part, :]
+            lat[pl.ds(slot_of(p) + half * H * FR, H, stride=FR), :] = piece
+
+    def hand_over(n, carry):
+        psend[n] = half_of(n, 1 - core).astype(BF16)
+        to_sibling(n).start()
+        return carry
+
+    def pass_on(n, carry):
+        two = (n // 4) * 4 + lax.rem(n + z, 4)
         to_sibling(two).wait_recv()
-        summed = (pmine[two] + precv[two].astype(F32)).astype(BF16)
+        summed = (half_of(two, core) + precv[two].astype(F32)).astype(BF16)
 
         @pl.when(jnp.logical_not(is_self(two)))
         def _():
@@ -462,15 +498,12 @@
         def _():
             lrecv[z] = summed
 
-    attend(0)
-
-    def attend_and_pass(n, carry):
-        attend(n)
-        pass_on(n - 1)
         return carry
 
-    lax.fori_loop(1, FR // 2, attend_and_pass, 0)
-    pass_on(FR // 2 - 1)
+    for half in range(2):
+        finish(half)
+        lax.fori_loop(half * 4, half * 4 + 4, hand_over, 0)
+        lax.fori_loop(half * 4, half * 4 + 4, pass_on, 0)
 
     def latent_wait(n, carry):
         here = jnp.logical_and(core == y_lo, lax.rem(t, 2) == core)
@@ -646,10 +679,9 @@
             pltpu.VMEM((NZ, 32, 256), BF16),
             pltpu.VMEM((3, 9 * LAT, CH), BF16),
             pltpu.VMEM((3, 9 * CH, CH), BF16),
-            pltpu.VMEM((FR * BLK, HD), F32),
+            pltpu.VMEM((FR, BLK, HD), BF16),
             pltpu.VMEM((HD, FR * BLK), BF16),
             pltpu.VMEM((FR * BLK, 2 * HD), BF16),
-            pltpu.VMEM((FR * BLK, LAT), F32),
             pltpu.VMEM((BLK, LAT), F32),
             pltpu.VMEM((BLK, LAT), F32),
             pltpu.VMEM((FR, 32, LAT), BF16),
@@ -659,10 +691,9 @@
             pltpu.VMEM((NZ, BLK, LAT), BF16),
             pltpu.VMEM((NZ, BLK, LAT), BF16),
             pltpu.VMEM((NZ, BLK, LAT), BF16),
-            pltpu.VMEM((NZ, BLK, LAT), F32),
-            pltpu.VMEM((FR * BLK, HD), F32),
-            pltpu.VMEM((FR * BLK, HD), F32),
-            pltpu.VMEM((FR * BLK, HD), F32),
+            pltpu.VMEM((FR * BLK, LAT), F32),
+            pltpu.VMEM((FR, BLK, HD), F32),
+            pltpu.VMEM((FR, BLK, 2 * HD), F32),
             pltpu.VMEM((4 * BLK, 4 * BLK), BF16),
             pltpu.VMEM((8, 6, FR, LAT), BF16),
             pltpu.VMEM((6, 4, FR, CH), BF16),

time: 131 us -> 125 us (0.954); the launches traced: 131 us -> 123 us
  Pallas kernels: 129 us -> 121 us
    pallas_call x1, Pallas kernels: 129 us -> 121 us  [shards(): pl.pallas_call(kernel, out_shape=jax.ShapeDtypeStruct((4 * BLK, CH), BF16...]
where the time goes in v4:
time: 125 us; the launch traced here: 123 us
  Pallas kernels  121 us (97%)
  local copies, waits for them, and re-layouts  1.72 us (1%)
    pallas_call x1, Pallas kernels, shards(): pl.pallas_call(kernel, out_shape=jax.ShapeDtypeStruct((4 * BLK, CH), BF16...  121 us

profile of v4, /device:TPU:7, one launch (start us, length us, event | category | flops | bytes accessed | tf_op | source)
XLA Modules:
  0.0 122.5 jit_solution(12375868630350904552)
XLA Ops:
  0.0 120.8 %shard_map.100 = bf16[512,256]{1,0:T(8,128)(2,1)} custom-call(bf16[128,4096]{1,0:T(8,128)(2,1)} %bitcast.11, f32[2,4096]{1,0:T(2,128)} %mod_ref.1, bf16[3,4096,128]{2,1,0:T(8,128)(2,1)} %bitcast.9, bf16[2,8,4,32,256]{4,3,2,1,0:T(8,128)(2,1)} %bitcast.12, f32[1,256]{1,0:T(1,128)} %bitcast.13, bf16[4096,128]{1,0:T(8,128)(2,1)} %lw_hbm.1, ...), custom_call_target="tpu_custom_call" | custom-call | flops 12999999488 | bytes 14000000 | tf_op jit(solution)/shard_map/pallas_call | solution.py:669
  120.8 1.7 %reshape.27 = bf16[16,8,4,256]{3,2,1,0:T(4,128)(2,1)} reshape(bf16[512,256]{1,0:T(8,128)(2,1)} %shard_map.100) | data formatting | bytes 524288 | tf_op jit(solution)/shard_map/reshape | solution.py:732

commit v5 on v4

--- a/solution.py
+++ b/solution.py
@@ -24,11 +24,11 @@
 
 
 def kernel(
-    tok_ref, mod_ref, w_hbm, ow_hbm, gate_ref, lw_hbm, cw_hbm, cb_ref, rw_hbm, rb_ref,
+    tok_hbm, mod_hbm, w_hbm, ow_hbm, gate_hbm, lw_hbm, cw_hbm, cb_hbm, rw_hbm, rb_hbm,
     out_ref,
-    xall, xown, wv, lw, ow, cw, rw, qs, kt, v2, rmine, rbuf, mrecv, msend, mfull,
-    lsend, lrecv, psend, precv, lat, tops, sums, order, ext, coarse, cols2,
-    local_sem, wloc_sem, swx_send, swx_recv, sww_send, sww_recv, swr_send, swr_recv,
+    tok_ref, mod_ref, gate_ref, cb_ref, rb_ref, xall, xown, wv, lw, ow, cw, rw, qs, kt, v2, rmine, rbuf, mrecv, msend, mfull,
+    lsend, lrecv, psend, precv, lat, tops, sums, order, ext, coarse, wc,
+    early_sem, local_sem, wloc_sem, swx_send, swx_recv, sww_send, sww_recv, swr_send, swr_recv,
     ring_send, ring_recv, sib_send, sib_recv, m_send, m_recv, mx_send, mx_recv,
     l_send, l_recv, p_send, p_recv, h_send, h_recv,
 ):
@@ -53,6 +53,14 @@
     outer = g + 2 * core - 1
     has_outer = jnp.logical_and(outer >= 0, outer < n_g)
 
+    early_loads = [
+        pltpu.make_async_copy(src, dst, early_sem.at[n])
+        for n, (src, dst) in enumerate(
+            ((tok_hbm, tok_ref), (mod_hbm, mod_ref), (gate_hbm, gate_ref), (cb_hbm, cb_ref), (rb_hbm, rb_ref))
+        )
+    ]
+    for load in early_loads:
+        load.start()
     ext[...] = jnp.zeros_like(ext)
 
     barrier = pltpu.get_barrier_semaphore()
@@ -72,7 +80,9 @@
 
     lax.fori_loop(0, FR, greet_row, 0)
     for step in range(1, 4):
-        greet(y_hi * (2 * n_x) + lax.rem(x + step, n_x) * 2 + core, t)
+        beside = y_hi * (2 * n_x) + lax.rem(x + step, n_x) * 2 + core
+        greet(beside, t)
+        greet(beside, (1 - y_lo) * NZ + z)
 
     @pl.when(swapped)
     def _():
@@ -90,7 +100,7 @@
         def _():
             greet(outer, t + 1)
 
-    guests = 2 * FR - 1 + 3 + jnp.where(swapped, 1, 0) + jnp.where(
+    guests = 2 * FR - 1 + 6 + jnp.where(swapped, 1, 0) + jnp.where(
         has_outer, 1 + jnp.where(t > 0, 1, 0) + jnp.where(t < FR - 1, 1, 0), 0
     )
 
@@ -211,6 +221,8 @@
         ring(1, 0, sub).start()
         share(z, sub).start()
 
+    for load in early_loads:
+        load.wait()
     for sub in range(SUBS):
         prepare(sub)
         if sub == 0:
@@ -240,7 +252,7 @@
 
     def fold_copy(other):
         return pltpu.make_async_remote_copy(
-            src_ref=msend.at[lax.rem(other, NZ)],
+            src_ref=msend.at[lax.rem(other, NZ), pl.ds(pl.multiple_of(other // NZ * 16, 16), 16)],
             dst_ref=mrecv.at[t],
             send_sem=m_send.at[other],
             recv_sem=m_recv.at[t],
@@ -258,15 +270,21 @@
         return carry
 
     def fold_rows(which):
-        return mfull.at[pl.ds(pl.multiple_of(which * 32, 32), 32)]
+        return mfull.at[pl.ds(pl.multiple_of(which * 16, 16), 16)]
+
+    share_no = x * 2 + y_lo
 
     def spread(step):
-        return pltpu.make_async_remote_copy(
-            src_ref=fold_rows(x),
-            dst_ref=fold_rows(x),
+        there = lax.rem(share_no + step, 8)
+        return pltpu.make_async_remote_copy(
+            src_ref=fold_rows(share_no),
+            dst_ref=fold_rows(share_no),
             send_sem=mx_send.at[step],
-            recv_sem=mx_recv.at[x],
-            device_id=(y_hi * (2 * n_x) + lax.rem(x + step, n_x) * 2 + core, t),
+            recv_sem=mx_recv.at[share_no],
+            device_id=(
+                y_hi * (2 * n_x) + there // 2 * 2 + core,
+                lax.rem(there, 2) * NZ + z,
+            ),
             device_id_type=MESH,
         )
 
@@ -335,26 +353,18 @@
         return summed * jnp.concatenate([shrink, shrink], axis=1) + added
 
     def fresh(low, high, upto):
-        def one(n, carry):
-            at = pl.ds(2 * n, 2)
-            top, summed = meet(qs[at].reshape(2 * BLK, HD), 0, upto)
-            tops[at] = top.reshape(2, BLK, HD)
-            sums[at] = summed.reshape(2, BLK, 2 * HD)
-            return carry
-
-        lax.fori_loop(low // 2, high // 2, one, 0)
-
-    def update(rows, low, high):
-        def one(n, carry):
-            at = pl.ds(2 * n, 2)
-            before = tops[at].reshape(2 * BLK, HD)
-            top, added = meet(qs[at].reshape(2 * BLK, HD), low, high, before)
-            summed = merged(sums[at].reshape(2 * BLK, 2 * HD), before, top, added)
-            tops[at] = top.reshape(2, BLK, HD)
-            sums[at] = summed.reshape(2, BLK, 2 * HD)
-            return carry
-
-        lax.fori_loop(0, rows // 2, one, 0)
+        rows = (high - low) * BLK
+        top, summed = meet(qs[low:high].reshape(rows, HD), 0, upto)
+        tops[low:high] = top.reshape(high - low, BLK, HD)
+        sums[low:high] = summed.reshape(high - low, BLK, 2 * HD)
+
+    def update(count, low, high):
+        rows = count * BLK
+        before = tops[0:count].reshape(rows, HD)
+        top, added = meet(qs[0:count].reshape(rows, HD), low, high, before)
+        summed = merged(sums[0:count].reshape(rows, 2 * HD), before, top, added)
+        tops[0:count] = top.reshape(count, BLK, HD)
+        sums[0:count] = summed.reshape(count, BLK, 2 * HD)
 
     forward(1, 0)
     v2[:, HD:] = jnp.ones((v2.shape[0], HD), BF16)
@@ -373,7 +383,7 @@
     part = jnp.dot(scaled, lw[cols, :], preferred_element_type=F32)
     msend[...] = part.astype(BF16).reshape(NZ, 32, LAT)
 
-    mrecv[t] = msend[z]
+    mrecv[t] = msend[z, pl.ds(pl.multiple_of(y_lo * 16, 16), 16), :]
 
     def fold_send(step, carry):
         fold_copy(lax.rem(t + step, FR)).start()
@@ -382,7 +392,27 @@
     lax.fori_loop(1, FR, fold_send, 0)
 
     forward(1, 2)
+
+    load_rw.wait()
+    taps = (((0,), (1, 2)), ((0, 1), (2,)))
+
+    def combine(p, q):
+        for a in range(3):
+            for u in range(2):
+                for v in range(2):
+                    total = jnp.zeros((CH, CH), F32)
+                    for b in taps[p][u]:
+                        for c in taps[q][v]:
+                            at = (b * 3 + c) * CH
+                            total = total + rw[a, at : at + CH, :].astype(F32)
+                    k = (u * 2 + v) * CH
+                    wc[p * 2 + q, k : k + CH, a * CH : (a + 1) * CH] = total.astype(BF16)
+
+    combine(0, 0)
+    combine(0, 1)
     forward(1, 3)
+    combine(1, 0)
+    combine(1, 1)
     forward(2, 0)
 
     @pl.when(jnp.logical_not(swapped))
@@ -411,8 +441,8 @@
     total = mrecv[0].astype(F32)
     for other in range(1, FR):
         total = total + mrecv[other].astype(F32)
-    mfull[pl.ds(pl.multiple_of(x * 32, 32), 32), :] = total.astype(BF16)
-    for step in range(1, 4):
+    mfull[pl.ds(pl.multiple_of(share_no * 16, 16), 16), :] = total.astype(BF16)
+    for step in range(1, 8):
         spread(step).start()
     forward(3, 1)
     project(1, 8, 10)
@@ -428,8 +458,8 @@
     forward(4, 2)
     update(10, 10, 14)
     fresh(10, 14, 14)
-    for step in range(1, 4):
-        there = lax.rem(x + step, n_x)
+    for step in range(1, 8):
+        there = lax.rem(share_no + step, 8)
         pltpu.make_async_copy(fold_rows(there), fold_rows(there), mx_recv.at[there]).wait()
     forward(4, 3)
     project(3, 14, 16)
@@ -545,7 +575,6 @@
             halo(dg, dt).start()
 
     load_cw.wait()
-    load_rw.wait()
     for dg, dt in ways:
 
         @pl.when(inside(-dg, -dt))
@@ -590,18 +619,23 @@
         coarse[:, 3:4] = jnp.zeros((6, 1, FR, CH), BF16)
 
     rows = 8 * FR
+    parts = []
     for p in range(2):
         for q in range(2):
-            for b in range(3):
-                for c in range(3):
-                    r0 = 1 + (p + b - 1) // 2
-                    c0 = 1 + (q + c - 1) // 2
-                    at = (p * 2 + q) * rows
-                    k = (b * 3 + c) * CH
-                    cols2[at : at + rows, k : k + CH] = coarse[
-                        r0 : r0 + 4, c0 : c0 + 2
-                    ].reshape(rows, CH)
-    three = [jnp.dot(cols2[...], rw[a], preferred_element_type=F32) for a in range(3)]
+            views = [
+                coarse[p + u : p + u + 4, q + v : q + v + 2].reshape(rows, CH)
+                for u in range(2)
+                for v in range(2)
+            ]
+            parts.append(
+                jnp.dot(
+                    jnp.concatenate(views, axis=1), wc[p * 2 + q], preferred_element_type=F32
+                )
+            )
+    three = [
+        jnp.concatenate([part[:, a * CH : (a + 1) * CH] for part in parts], axis=0)
+        for a in range(3)
+    ]
     mixed = over_frames(three, 4 * rows)
     center = coarse[1:5, 1:3].reshape(rows, CH).astype(F32)
     center = jnp.concatenate([center] * 4, axis=0)
@@ -631,7 +665,7 @@
         swap_r().wait_send()
 
     lax.fori_loop(1, FR, fold_sent, 0)
-    for step in range(1, 4):
+    for step in range(1, 8):
         spread(step).wait_send()
 
     def latent_sent(two, carry):
@@ -669,9 +703,14 @@
     out = pl.pallas_call(
         kernel,
         out_shape=jax.ShapeDtypeStruct((4 * BLK, CH), BF16),
-        in_specs=[vmem, vmem, hbm, hbm, vmem, hbm, hbm, vmem, hbm, vmem],
+        in_specs=[hbm] * 10,
         out_specs=vmem,
         scratch_shapes=[
+            pltpu.VMEM((BLK, D), BF16),
+            pltpu.VMEM((2, D), F32),
+            pltpu.VMEM((1, 256), F32),
+            pltpu.VMEM((1, CH), F32),
+            pltpu.VMEM((1, CH), F32),
             pltpu.VMEM((FR, BLK, D), BF16),
             pltpu.VMEM((BLK, D), BF16),
             pltpu.VMEM((D, 3 * HD), BF16),
@@ -684,7 +723,7 @@
             pltpu.VMEM((FR * BLK, 2 * HD), BF16),
             pltpu.VMEM((BLK, LAT), F32),
             pltpu.VMEM((BLK, LAT), F32),
-            pltpu.VMEM((FR, 32, LAT), BF16),
+            pltpu.VMEM((FR, 16, LAT), BF16),
             pltpu.VMEM((NZ, 32, LAT), BF16),
             pltpu.VMEM((HD, LAT), BF16),
             pltpu.VMEM((NZ, BLK, LAT), BF16),
@@ -697,7 +736,8 @@
             pltpu.VMEM((4 * BLK, 4 * BLK), BF16),
             pltpu.VMEM((8, 6, FR, LAT), BF16),
             pltpu.VMEM((6, 4, FR, CH), BF16),
-            pltpu.VMEM((4 * 8 * FR, 9 * CH), BF16),
+            pltpu.VMEM((4, 4 * CH, 3 * CH), BF16),
+            dma((5,)),
             dma((4,)),
             dma((3,)),
             dma((SUBS,)), dma((SUBS,)),
@@ -706,7 +746,7 @@
             dma((2, 4, SUBS)), dma((2, 4, SUBS)),
             dma((NZ, SUBS)), dma((NZ, SUBS)),
             dma((FR,)), dma((FR,)),
-            dma((4,)), dma((4,)),
+            dma((8,)), dma((8,)),
             dma((NZ,)), dma((NZ,)),
             dma((NZ,)), dma((NZ,)),
             dma((9,)), dma((9,)),

time: 125 us -> 119 us (0.952)
  Pallas kernels: 121 us -> 115 us
    pallas_call x1, Pallas kernels: 121 us -> 115 us  [shards(): pl.pallas_call(kernel, out_shape=jax.ShapeDtypeStruct((4 * BLK, CH), BF16...]
where the time goes in v5:
time: 119 us; the launch traced here: 117 us
  Pallas kernels  115 us (97%)
  local copies, waits for them, and re-layouts  1.72 us (1%)
    pallas_call x1, Pallas kernels, shards(): pl.pallas_call(kernel, out_shape=jax.ShapeDtypeStruct((4 * BLK, CH), BF16...  115 us

profile of v5, /device:TPU:7, one launch (start us, length us, event | category | flops | bytes accessed | tf_op | source)
XLA Modules:
  0.0 117.0 jit_solution(8918993760459318357)
XLA Ops:
  0.0 115.2 %shard_map.100 = bf16[512,256]{1,0:T(8,128)(2,1)} custom-call(bf16[128,4096]{1,0:T(8,128)(2,1)} %bitcast.11, f32[2,4096]{1,0:T(2,128)} %mod_hbm.1, bf16[3,4096,128]{2,1,0:T(8,128)(2,1)} %bitcast.9, bf16[2,8,4,32,256]{4,3,2,1,0:T(8,128)(2,1)} %bitcast.12, f32[1,256]{1,0:T(1,128)} %bitcast.13, bf16[4096,128]{1,0:T(8,128)(2,1)} %lw_hbm.1, ...), custom_call_target="tpu_custom_call" | custom-call | flops 12999999488 | bytes 14000000 | tf_op jit(solution)/shard_map/pallas_call | solution.py:703
  115.2 1.7 %reshape.27 = bf16[16,8,4,256]{3,2,1,0:T(4,128)(2,1)} reshape(bf16[512,256]{1,0:T(8,128)(2,1)} %shard_map.100) | data formatting | bytes 524288 | tf_op jit(solution)/shard_map/reshape | solution.py:772

commit v6 on v5

--- a/solution.py
+++ b/solution.py
@@ -453,11 +453,11 @@
 
     forward(4, 0)
     project(2, 10, 12)
-    forward(4, 1)
     project(2, 12, 14)
-    forward(4, 2)
     update(10, 10, 14)
     fresh(10, 14, 14)
+    forward(4, 1)
+    forward(4, 2)
     for step in range(1, 8):
         there = lax.rem(share_no + step, 8)
         pltpu.make_async_copy(fold_rows(there), fold_rows(there), mx_recv.at[there]).wait()
@@ -535,6 +535,32 @@
         lax.fori_loop(half * 4, half * 4 + 4, hand_over, 0)
         lax.fori_loop(half * 4, half * 4 + 4, pass_on, 0)
 
+    for sub in range(SUBS):
+
+        @pl.when(swapped)
+        def _():
+            swap_x(sub).wait_send()
+
+        for way in range(2):
+            for step in range(4):
+
+                @pl.when(step < reach[way])
+                def _():
+                    ring(way, step, sub).wait_send()
+
+        for origin in range(NZ):
+            share(origin, sub).wait_send()
+
+    @pl.when(swapped)
+    def _():
+        for k in range(3):
+            swap_w(k).wait_send()
+        swap_r().wait_send()
+
+    lax.fori_loop(1, FR, fold_sent, 0)
+    for step in range(1, 8):
+        spread(step).wait_send()
+
     def latent_wait(n, carry):
         here = jnp.logical_and(core == y_lo, lax.rem(t, 2) == core)
 
@@ -574,6 +600,16 @@
         def _():
             halo(dg, dt).start()
 
+    def latent_sent(two, carry):
+        to_sibling(two).wait_send()
+
+        @pl.when(jnp.logical_not(is_self(two)))
+        def _():
+            latent_copy(two).wait_send()
+
+        return carry
+
+    lax.fori_loop(0, FR // 2, latent_sent, 0)
     load_cw.wait()
     for dg, dt in ways:
 
@@ -642,42 +678,6 @@
     result = silu(center + mixed + rb_ref[...]).astype(BF16)
     out_ref[...] = jnp.dot(order[...], result, preferred_element_type=F32).astype(BF16)
 
-    for sub in range(SUBS):
-
-        @pl.when(swapped)
-        def _():
-            swap_x(sub).wait_send()
-
-        for way in range(2):
-            for step in range(4):
-
-                @pl.when(step < reach[way])
-                def _():
-                    ring(way, step, sub).wait_send()
-
-        for origin in range(NZ):
-            share(origin, sub).wait_send()
-
-    @pl.when(swapped)
-    def _():
-        for k in range(3):
-            swap_w(k).wait_send()
-        swap_r().wait_send()
-
-    lax.fori_loop(1, FR, fold_sent, 0)
-    for step in range(1, 8):
-        spread(step).wait_send()
-
-    def latent_sent(two, carry):
-        to_sibling(two).wait_send()
-
-        @pl.when(jnp.logical_not(is_self(two)))
-        def _():
-            latent_copy(two).wait_send()
-
-        return carry
-
-    lax.fori_loop(0, FR // 2, latent_sent, 0)
     for dg, dt in ways:
 
         @pl.when(inside(dg, dt))

time: 119 us -> 119 us (level)
  no operation moved by 1% of the time
where the time goes in v6:
time: 119 us; the launch traced here: 118 us
  Pallas kernels  116 us (97%)
  local copies, waits for them, and re-layouts  1.72 us (1%)
    pallas_call x1, Pallas kernels, shards(): pl.pallas_call(kernel, out_shape=jax.ShapeDtypeStruct((4 * BLK, CH), BF16...  116 us

profile of v6, /device:TPU:7, one launch (start us, length us, event | category | flops | bytes accessed | tf_op | source)
XLA Modules:
  0.0 118.1 jit_solution(13843646172610661179)
XLA Ops:
  0.0 116.4 %shard_map.100 = bf16[512,256]{1,0:T(8,128)(2,1)} custom-call(bf16[128,4096]{1,0:T(8,128)(2,1)} %bitcast.11, f32[2,4096]{1,0:T(2,128)} %mod_hbm.1, bf16[3,4096,128]{2,1,0:T(8,128)(2,1)} %bitcast.9, bf16[2,8,4,32,256]{4,3,2,1,0:T(8,128)(2,1)} %bitcast.12, f32[1,256]{1,0:T(1,128)} %bitcast.13, bf16[4096,128]{1,0:T(8,128)(2,1)} %lw_hbm.1, ...), custom_call_target="tpu_custom_call" | custom-call | flops 12999999488 | bytes 14000000 | tf_op jit(solution)/shard_map/pallas_call | solution.py:703
  116.4 1.7 %reshape.27 = bf16[16,8,4,256]{3,2,1,0:T(4,128)(2,1)} reshape(bf16[512,256]{1,0:T(8,128)(2,1)} %shard_map.100) | data formatting | bytes 524288 | tf_op jit(solution)/shard_map/reshape | solution.py:772

commit v7 on v6

--- a/solution.py
+++ b/solution.py
@@ -238,17 +238,20 @@
         def _():
             depart(sub)
 
+    @pl.when(swapped)
+    def _():
+        swap_w(2).start()
+        for sub in range(SUBS):
+            wait_swap_x(sub)
+            depart(sub)
+
     load_lw.wait()
     own_rows = jnp.dot(pick, tok_ref[...], preferred_element_type=F32).astype(BF16)
     rmine[...] = jnp.dot(own_rows, lw[...], preferred_element_type=F32)
 
     @pl.when(swapped)
     def _():
-        swap_w(2).start()
         swap_r().start()
-        for sub in range(SUBS):
-            wait_swap_x(sub)
-            depart(sub)
 
     def fold_copy(other):
         return pltpu.make_async_remote_copy(

time: 119 us -> 119 us (level)
  no operation moved by 1% of the time
where the time goes in v7:
time: 119 us; the launch traced here: 118 us
  Pallas kernels  116 us (97%)
  local copies, waits for them, and re-layouts  1.72 us (1%)
    pallas_call x1, Pallas kernels, shards(): pl.pallas_call(kernel, out_shape=jax.ShapeDtypeStruct((4 * BLK, CH), BF16...  116 us

profile of v7, /device:TPU:7, one launch (start us, length us, event | category | flops | bytes accessed | tf_op | source)
XLA Modules:
  0.0 118.1 jit_solution(5399289189386693628)
XLA Ops:
  0.0 116.4 %shard_map.100 = bf16[512,256]{1,0:T(8,128)(2,1)} custom-call(bf16[128,4096]{1,0:T(8,128)(2,1)} %bitcast.11, f32[2,4096]{1,0:T(2,128)} %mod_hbm.1, bf16[3,4096,128]{2,1,0:T(8,128)(2,1)} %bitcast.9, bf16[2,8,4,32,256]{4,3,2,1,0:T(8,128)(2,1)} %bitcast.12, f32[1,256]{1,0:T(1,128)} %bitcast.13, bf16[4096,128]{1,0:T(8,128)(2,1)} %lw_hbm.1, ...), custom_call_target="tpu_custom_call" | custom-call | flops 12999999488 | bytes 14000000 | tf_op jit(solution)/shard_map/pallas_call | solution.py:706
  116.4 1.7 %reshape.27 = bf16[16,8,4,256]{3,2,1,0:T(4,128)(2,1)} reshape(bf16[512,256]{1,0:T(8,128)(2,1)} %shard_map.100) | data formatting | bytes 524288 | tf_op jit(solution)/shard_map/reshape | solution.py:775
